TPU v7x, 32 devices: a whole 2x2x4 slice. The times are simulated.
32 devices in a mesh: view: 4 (over x, core), dp: 8 (over z, y).
Axes of the slice: x: 2, y: 2, z: 4, core: 2. Of those that a mesh axis runs over, the one named last changes fastest.
Arguments:
- tokens: bfloat16 [4, 10368, 768], P('view', 'dp'), may hold values from -6 to 6
- item_class: int32 [32], P('dp'), may hold values from 0 to 2, as said below
- norm_gain: float32 [4, 3, 768], P('view'), may hold values from 0.5 to 1.5
- norm_bias: float32 [4, 3, 768], P('view'), may hold values from -1.75 to 1.75
- attn_qkv: bfloat16 [4, 768, 2304], P('view'), may hold values from -0.21875 to 0.21875
- attn_out: bfloat16 [4, 768, 768], P('view'), may hold values from -0.875 to 0.875
- mlp_up: bfloat16 [4, 768, 3072], P('view'), may hold values from -0.21875 to 0.21875
- mlp_down: bfloat16 [4, 3072, 768], P('view'), may hold values from -0.109375 to 0.109375
- join_query: bfloat16 [4, 768, 768], P('view'), may hold values from -0.21875 to 0.21875
- join_keyval: bfloat16 [4, 768, 1536], P('view'), may hold values from -0.21875 to 0.21875
- join_output: bfloat16 [4, 768, 768], P('view'), may hold values from -0.875 to 0.875
- cotangent: bfloat16 [4, 10368, 768], P('view', 'dp'), may hold values from -6 to 6
Outputs:
- joined_tokens: bfloat16 [4, 10368, 768], P('view', 'dp')
- grad_tokens: float32 [4, 10368, 768], P('view', 'dp')
- grad_norm_gain: float32 [4, 3, 768], P('view', None, 'dp')
- grad_norm_bias: float32 [4, 3, 768], P('view', None, 'dp')
- grad_attn_qkv: float32 [4, 768, 2304], P('view', 'dp')
- grad_attn_out: float32 [4, 768, 768], P('view', 'dp')
- grad_mlp_up: float32 [4, 768, 3072], P('view', 'dp')
- grad_mlp_down: float32 [4, 3072, 768], P('view', 'dp')
- grad_join_query: float32 [4, 768, 768], P('view', 'dp')
- grad_join_keyval: float32 [4, 768, 1536], P('view', 'dp')
- grad_join_output: float32 [4, 768, 768], P('view', 'dp')
Inputs may be any that keep to these rules, and one draw needn't show every extreme that they name: `item_class`: each clip's resolution class; class 2 and class 0 both occur in every draw.
All inputs are finite; a program needn't handle non-finite values.
Results may differ from a plain program's by a relative error of at most 0.024.
Values may be sent and summed in bfloat16 or wider, within the bound.
No kernel may reach another device: no remote copies, remote signals or barrier semaphores. Data moves between devices by JAX's collectives and lax.ppermute only.
A program may use at most 320 MiB of HBM per device.

v0:
```python
import jax
import jax.numpy as jnp
from jax import lax
from jax.sharding import PartitionSpec as P

HEADS = 12
SIDE_BASE = 10
SIDE_STEP = 4
SLOT = 324


def shifted(value, axis, steps):
    count = lax.axis_size(axis)
    pairs = [(source, (source + steps) % count) for source in range(count)]
    return lax.ppermute(value, axis, pairs)


def norm_rows(values, gain_row, bias_row):
    centre = jnp.mean(values, -1, keepdims=True)
    centred = values - centre
    spread = jnp.mean(centred * centred, -1, keepdims=True)
    return centred * lax.rsqrt(spread + 1e-05) * gain_row + bias_row


def valid_slots(classes):
    sides = SIDE_BASE + SIDE_STEP * classes
    places = jnp.arange(SLOT, dtype=jnp.int32)
    return places[None, :] < (sides * sides)[:, None]


def reshape_into_heads(rows, count):
    return rows.reshape(count, SLOT, HEADS, rows.shape[1] // HEADS)


def score_block(query_heads, key_heads, valid):
    scale = query_heads.shape[3] ** (-0.5)
    scores = (
        jnp.einsum("cqhd,ckhd->chqk", query_heads, key_heads, preferred_element_type=jnp.float32)
        * scale
    )
    return jnp.where(valid[:, None, None, :], scores, -1e30)


def attend(query_rows, key_rows, value_rows, valid):
    count = valid.shape[0]
    query_heads = reshape_into_heads(query_rows, count)
    key_heads = reshape_into_heads(key_rows, count)
    value_heads = reshape_into_heads(value_rows, count)
    scores = score_block(query_heads, key_heads, valid)
    largest = jnp.max(scores, -1, keepdims=True)
    exp_scores = jnp.exp(scores - largest)
    totals = jnp.sum(exp_scores, -1, keepdims=True)
    probs = (exp_scores / totals).astype(jnp.bfloat16)
    mixed = jnp.einsum("chqk,ckhd->cqhd", probs, value_heads, preferred_element_type=jnp.float32)
    return (mixed.reshape(query_rows.shape[0], -1), largest + jnp.log(totals))


def attend_back(query_rows, key_rows, value_rows, valid, log_totals, grad_mixed):
    count = valid.shape[0]
    scale = (query_rows.shape[1] // HEADS) ** (-0.5)
    query_heads = reshape_into_heads(query_rows, count)
    key_heads = reshape_into_heads(key_rows, count)
    value_heads = reshape_into_heads(value_rows, count)
    grad_heads = reshape_into_heads(grad_mixed, count)
    scores = score_block(query_heads, key_heads, valid)
    probs_full = jnp.exp(scores - log_totals)
    probs_low = probs_full.astype(jnp.bfloat16)
    grad_probs = jnp.einsum(
        "cqhd,ckhd->chqk", grad_heads, value_heads, preferred_element_type=jnp.float32
    )
    row_terms = jnp.sum(probs_full * grad_probs, -1, keepdims=True)
    grad_scores = (probs_full * (grad_probs - row_terms)).astype(jnp.bfloat16)
    grad_query = (
        jnp.einsum("chqk,ckhd->cqhd", grad_scores, key_heads, preferred_element_type=jnp.float32)
        * scale
    )
    grad_key = (
        jnp.einsum("chqk,cqhd->ckhd", grad_scores, query_heads, preferred_element_type=jnp.float32)
        * scale
    )
    grad_value = jnp.einsum(
        "chqk,cqhd->ckhd", probs_low, grad_heads, preferred_element_type=jnp.float32
    )
    rows = query_rows.shape[0]
    return (grad_query.reshape(rows, -1), grad_key.reshape(rows, -1), grad_value.reshape(rows, -1))


def matmul(left_neighbour_view, right_neighbour_view):
    return jnp.dot(left_neighbour_view, right_neighbour_view, preferred_element_type=jnp.float32)


def weight_grad(left_neighbour_view, right_neighbour_view):
    return jnp.einsum(
        "rd,re->de", left_neighbour_view, right_neighbour_view, preferred_element_type=jnp.float32
    )


def gradient_wrt_input(grad_rows, weight):
    return jnp.einsum("re,de->rd", grad_rows, weight, preferred_element_type=jnp.float32)


def per_device(
    tokens,
    item_class,
    norm_gain,
    norm_bias,
    attn_qkv,
    attn_out,
    mlp_up,
    mlp_down,
    join_query,
    join_keyval,
    join_output,
    cotangent,
):
    width = tokens.shape[2]
    valid = valid_slots(item_class)
    live_rows = valid.reshape(-1).astype(jnp.float32)[:, None]
    inputs = tokens[0].astype(jnp.float32)
    gains = norm_gain[0]
    biases = norm_bias[0]
    weight_qkv = attn_qkv[0]
    weight_out = attn_out[0]
    weight_up = mlp_up[0]
    weight_down = mlp_down[0]
    weight_fq = join_query[0]
    weight_fkv = join_keyval[0]
    weight_fo = join_output[0]
    normed_one, norm_back_one = jax.vjp(norm_rows, inputs, gains[0], biases[0])
    low_one = normed_one.astype(jnp.bfloat16)
    triple = matmul(low_one, weight_qkv).astype(jnp.bfloat16)
    query_rows = triple[:, :width]
    key_rows = triple[:, width : 2 * width]
    value_rows = triple[:, 2 * width :]
    mixed_one, logsum_one = attend(query_rows, key_rows, value_rows, valid)
    mixed_low = mixed_one.astype(jnp.bfloat16)
    middle = inputs + matmul(mixed_low, weight_out)
    normed_two, norm_back_two = jax.vjp(norm_rows, middle, gains[1], biases[1])
    low_two = normed_two.astype(jnp.bfloat16)
    hidden = matmul(low_two, weight_up)
    activated, gelu_back = jax.vjp(jax.nn.gelu, hidden)
    act_low = activated.astype(jnp.bfloat16)
    layer_one = middle + matmul(act_low, weight_down)
    normed_three, norm_back_three = jax.vjp(norm_rows, layer_one, gains[2], biases[2])
    low_three = normed_three.astype(jnp.bfloat16)
    join_queries = matmul(low_three, weight_fq).astype(jnp.bfloat16)
    join_pairs = matmul(low_three, weight_fkv).astype(jnp.bfloat16)
    arrived = shifted(join_pairs, "view", -1)
    join_keys = arrived[:, :width]
    join_values = arrived[:, width:]
    join_mixed, join_logsum = attend(join_queries, join_keys, join_values, valid)
    join_low = join_mixed.astype(jnp.bfloat16)
    result = (layer_one + matmul(join_low, weight_fo)) * live_rows
    joined_tokens = result.astype(jnp.bfloat16)[None]
    grad_result = cotangent[0].astype(jnp.float32) * live_rows
    grad_result_low = grad_result.astype(jnp.bfloat16)
    grad_fo = weight_grad(join_low, grad_result_low)
    grad_join_mixed = gradient_wrt_input(grad_result_low, weight_fo).astype(jnp.bfloat16)
    grad_fq_rows, grad_fk_rows, grad_fv_rows = attend_back(
        join_queries, join_keys, join_values, valid, join_logsum, grad_join_mixed
    )
    grad_fq_low = grad_fq_rows.astype(jnp.bfloat16)
    grad_pairs = jnp.concatenate([grad_fk_rows, grad_fv_rows], axis=1).astype(jnp.bfloat16)
    returned = shifted(grad_pairs, "view", 1)
    grad_fq = weight_grad(low_three, grad_fq_low)
    grad_joining_keyvalue_weight = weight_grad(low_three, returned)
    grad_normed_three = gradient_wrt_input(grad_fq_low, weight_fq) + gradient_wrt_input(
        returned, weight_fkv
    )
    grad_layer_norm, gain_three, bias_three = norm_back_three(grad_normed_three)
    grad_layer = grad_result + grad_layer_norm
    down_low = grad_layer.astype(jnp.bfloat16)
    grad_down = weight_grad(act_low, down_low)
    grad_act = gradient_wrt_input(down_low, weight_down)
    grad_hidden = gelu_back(grad_act)[0]
    hidden_low = grad_hidden.astype(jnp.bfloat16)
    grad_up = weight_grad(low_two, hidden_low)
    grad_middle_norm, gain_two, bias_two = norm_back_two(gradient_wrt_input(hidden_low, weight_up))
    grad_middle = grad_layer + grad_middle_norm
    out_low = grad_middle.astype(jnp.bfloat16)
    grad_out_weight = weight_grad(mixed_low, out_low)
    grad_mixed = gradient_wrt_input(out_low, weight_out).astype(jnp.bfloat16)
    grad_query, grad_key, grad_value = attend_back(
        query_rows, key_rows, value_rows, valid, logsum_one, grad_mixed
    )
    triple_grad = jnp.concatenate([grad_query, grad_key, grad_value], axis=1).astype(jnp.bfloat16)
    grad_qkv = weight_grad(low_one, triple_grad)
    grad_input_norm, gain_one, bias_one = norm_back_one(gradient_wrt_input(triple_grad, weight_qkv))
    grad_inputs = grad_middle + grad_input_norm
    gain_grads = jnp.stack([gain_one, gain_two, gain_three])[None]
    bias_grads = jnp.stack([bias_one, bias_two, bias_three])[None]
    all_sums = (
        lax.psum_scatter(grad_qkv[None], "dp", scatter_dimension=1, tiled=True),
        lax.psum_scatter(grad_out_weight[None], "dp", scatter_dimension=1, tiled=True),
        lax.psum_scatter(grad_up[None], "dp", scatter_dimension=1, tiled=True),
        lax.psum_scatter(grad_down[None], "dp", scatter_dimension=1, tiled=True),
        lax.psum_scatter(grad_fq[None], "dp", scatter_dimension=1, tiled=True),
        lax.psum_scatter(grad_joining_keyvalue_weight[None], "dp", scatter_dimension=1, tiled=True),
        lax.psum_scatter(grad_fo[None], "dp", scatter_dimension=1, tiled=True),
        lax.psum_scatter(gain_grads, "dp", scatter_dimension=2, tiled=True),
        lax.psum_scatter(bias_grads, "dp", scatter_dimension=2, tiled=True),
    )
    sum_qkv, sum_out, sum_up, sum_down, sum_fq, sum_fkv, sum_fo, sum_gain, sum_bias = all_sums
    return (
        joined_tokens,
        grad_inputs[None],
        sum_gain,
        sum_bias,
        sum_qkv,
        sum_out,
        sum_up,
        sum_down,
        sum_fq,
        sum_fkv,
        sum_fo,
    )


def solution(mesh):
    return jax.shard_map(
        per_device,
        mesh=mesh,
        in_specs=(
            P("view", "dp", None),
            P("dp"),
            P("view", None, None),
            P("view", None, None),
            P("view", None, None),
            P("view", None, None),
            P("view", None, None),
            P("view", None, None),
            P("view", None, None),
            P("view", None, None),
            P("view", None, None),
            P("view", "dp", None),
        ),
        out_specs=(
            P("view", "dp", None),
            P("view", "dp", None),
            P("view", None, "dp"),
            P("view", None, "dp"),
            P("view", "dp", None),
            P("view", "dp", None),
            P("view", "dp", None),
            P("view", "dp", None),
            P("view", "dp", None),
            P("view", "dp", None),
            P("view", "dp", None),
        ),
        check_vma=False,
    )
```

profile of v0, /device:TPU:0, one launch (start us, length us, event | category | flops | bytes accessed | tf_op | source)
XLA Modules:
  0.0 1480.2 jit_solution(1387227275358759252)
XLA Ops:
  26.3 5.9 reshape.296
  36.3 5.9 reshape.298
  46.3 6.1 reshape.297
  52.4 17.0 %fusion.19 = (f32[4,12,324]{2,1,0:T(8,128)S(1)}, f32[4,12,324,324]{2,3,1,0:T(8,128)}) fusion(pred[4,324]{1,0:T(4,128)(4,1)S(1)} %get-tuple-element.37, bf16[4,324,12,64]{1,0,3,2:T(4,128)(2,1)} %reshape.298, bf16[4,324,12,64]{1,0,3,2:T(4,128)(2,1)} %reshape.297), kind=kOutput, calls=%fused_computation.33 | convolution fusion | flops 660073536 | bytes 24200208 | tf_op jit(solution)/shard_map/cqhd,ckhd->chqk/dot_general | solution.py:38
  69.3 11.6 fusion
  81.0 11.6 convert_bitcast_fusion.5
  106.2 13.6 fusion.35
  119.8 15.5 %fusion.139 = (f32[1296]{0:T(1024)S(1)}, f32[1296,768]{1,0:T(8,128)S(1)}) fusion(f32[1296,768]{1,0:T(8,128)S(1)} %get-tuple-element.41, bf16[1,3072,768]{2,1,0:T(8,128)(2,1)S(1)} %bitcast.200, f32[1296,3072]{1,0:T(8,128)} %fusion.35), kind=kOutput, calls=%fused_computation.204 | convolution fusion | flops 6153116160 | bytes 28611648 | tf_op jit(solution)/shard_map/dot_general | solution.py:89
  155.8 5.9 reshape.302
  170.7 5.9 reshape.300
  178.2 11.8 collective-permute-done
  198.5 5.9 reshape.299
  208.5 6.1 reshape.301
  214.6 17.0 %fusion.20 = (f32[4,12,324]{2,1,0:T(8,128)S(1)}, f32[4,12,324,324]{2,3,1,0:T(8,128)}) fusion(pred[4,324]{1,0:T(4,128)(4,1)S(1)} %get-tuple-element.37, bf16[4,324,12,64]{1,0,3,2:T(4,128)(2,1)} %reshape.301, bf16[4,324,12,64]{1,0,3,2:T(4,128)(2,1)} %reshape.300), kind=kOutput, calls=%fused_computation.34 | convolution fusion | flops 660073536 | bytes 24200208 | tf_op jit(solution)/shard_map/cqhd,ckhd->chqk/dot_general | solution.py:38
  231.6 11.6 fusion.1
  244.5 11.3 convert_bitcast_fusion.3
  264.2 19.7 %multiply_reduce_fusion.1 = (f32[4,12,324]{2,1,0:T(8,128)}, f32[4,12,324,324]{2,3,1,0:T(8,128)}) fusion(f32[4,12,324]{2,1,0:T(8,128)} %log_add_fusion.1, f32[4,12,324,324]{2,3,1,0:T(8,128)} %get-tuple-element.45, pred[4,324]{1,0:T(4,128)(4,1)S(1)} %get-tuple-element.37, bf16[4,324,12,64]{1,0,3,2:T(4,128)(2,1)} %reshape.299, ...), kind=kOutput, calls=%fused_computation.4 | convolution fusion | flops 670151232 | bytes 44417808 | tf_op jit(solution)/shard_map/cqhd,ckhd->chqk/dot_general | solution.py:68
  283.9 20.9 %multiply_convert_fusion.1 = bf16[4,12,324,324]{2,3,1,0:T(8,128)(2,1)} fusion(f32[4,12,324,324]{2,3,1,0:T(8,128)} %get-tuple-element.47, f32[4,12,324]{2,1,0:T(8,128)} %get-tuple-element.46, f32[4,12,324]{2,1,0:T(8,128)} %log_add_fusion.1, f32[4,12,324,324]{2,3,1,0:T(8,128)} %get-tuple-element.45, pred[4,324]{1,0:T(4,128)(4,1)S(1)} %get-tuple-element.37), kind=kLoop, calls=%fused_computation.3 | loop fusion | flops 30233088 | bytes 50514192 | tf_op jit(solution)/shard_map/convert_element_type | solution.py:72
  304.8 10.3 fusion.59
  329.7 6.4 copy.115
  336.9 12.3 convert_bitcast_fusion.4
  357.6 7.5 fusion.58
  382.2 6.5 multiply_reduce_fusion.2
  392.4 18.4 %fusion.10 = bf16[1296,3072]{1,0:T(8,128)(2,1)} fusion(f32[1296,3072]{1,0:T(8,128)} %fusion.35, bf16[1296,768]{1,0:T(8,128)(2,1)S(1)} %fusion.64, bf16[1,3072,768]{2,1,0:T(8,128)(2,1)S(1)} %bitcast.202), kind=kOutput, calls=%fused_computation.24 | convolution fusion | flops 6194921472 | bytes 30597120 | tf_op jit(solution)/shard_map/re,de->rd/dot_general | solution.py:99
  410.8 12.8 multiply_reduce_fusion.3
  435.4 5.9 reshape.305
  441.3 12.8 convert_bitcast_fusion.2
  454.1 19.7 %multiply_reduce_fusion = (f32[4,12,324]{2,1,0:T(8,128)}, f32[4,12,324,324]{2,3,1,0:T(8,128)}) fusion(f32[4,12,324]{2,1,0:T(8,128)} %log_add_fusion, f32[4,12,324,324]{2,3,1,0:T(8,128)} %get-tuple-element.39, pred[4,324]{1,0:T(4,128)(4,1)S(1)} %get-tuple-element.37, bf16[4,324,12,64]{1,0,3,2:T(4,128)(2,1)} %reshape.296, bf16[4,324,12,64]{1,0,3,2:T(4,128)(2,1)} %reshape.305), kind=kOutput, calls=%fused_computation.1 | convolution fusion | flops 670151232 | bytes 44417808 | tf_op jit(solution)/shard_map/cqhd,ckhd->chqk/dot_general | solution.py:68
  473.9 21.1 %multiply_convert_fusion = bf16[4,12,324,324]{2,3,1,0:T(8,128)(2,1)} fusion(f32[4,12,324,324]{2,3,1,0:T(8,128)} %get-tuple-element.51, f32[4,12,324]{2,1,0:T(8,128)} %get-tuple-element.50, f32[4,12,324]{2,1,0:T(8,128)} %log_add_fusion, f32[4,12,324,324]{2,3,1,0:T(8,128)} %get-tuple-element.39, pred[4,324]{1,0:T(4,128)(4,1)S(1)} %get-tuple-element.37), kind=kLoop, calls=%fused_computation | loop fusion | flops 30233088 | bytes 50514192 | tf_op jit(solution)/shard_map/convert_element_type | solution.py:72
  494.9 10.3 fusion.61
  505.3 9.1 fusion.60
  549.7 6.2 fusion.133
  570.8 5.7 convolution_bitcast_fusion.4
  576.6 5.7 convolution_bitcast_fusion.5
  582.4 6.2 convolution_bitcast_fusion.6
  588.7 8.9 convolution_bitcast_fusion.3
  597.6 12.1 convolution_bitcast_fusion.1
  609.8 16.1 %convolution_bitcast_fusion = f32[1,3072,768]{2,1,0:T(8,128)} fusion(bf16[1296,768]{1,0:T(8,128)(2,1)} %copy-done.19, f32[1296,3072]{1,0:T(8,128)} %fusion.35), kind=kOutput, calls=%fused_computation.42 | convolution fusion | flops 6151127040 | bytes 27353088 | tf_op jit(solution)/shard_map/rd,re->de/dot_general | solution.py:93
  626.0 14.4 convolution_bitcast_fusion.2
  640.5 6.4 fusion.57
  653.0 38.0 %reduce-scatter.30.cloned.1.call-done = f32[96,3]{1,0:T(8,128)} async-done(((f32[768,3]{1,0:T(8,128)}), f32[96,3]{1,0:T(8,128)}) %reduce-scatter.30.cloned.1.call-update) | async-done | bytes 1168
  694.2 69.1 %reduce-scatter.26.cloned.1.call-done = f32[1,96,768]{2,1,0:T(8,128)} async-done(((f32[1,768,768]{2,1,0:T(8,128)}), f32[1,96,768]{2,1,0:T(8,128)}) %reduce-scatter.26.cloned.1.call-update) | async-done | bytes 294928 | tf_op jit(solution)/shard_map/reduce_scatter | solution.py:199
  763.3 72.1 %reduce-scatter.22.cloned.1.call-done = f32[1,96,768]{2,1,0:T(8,128)} async-done(((f32[1,768,768]{2,1,0:T(8,128)}), f32[1,96,768]{2,1,0:T(8,128)}) %reduce-scatter.22.cloned.1.call-update) | async-done | bytes 294928 | tf_op jit(solution)/shard_map/reduce_scatter | solution.py:197
  835.4 72.1 %reduce-scatter.16.cloned.1.call-done = f32[1,96,768]{2,1,0:T(8,128)} async-done(((f32[1,768,768]{2,1,0:T(8,128)}), f32[1,96,768]{2,1,0:T(8,128)}) %reduce-scatter.16.cloned.1.call-update) | async-done | bytes 294928 | tf_op jit(solution)/shard_map/reduce_scatter | solution.py:194
  907.5 98.5 %reduce-scatter.24.cloned.1.call-done = f32[1,96,1536]{2,1,0:T(8,128)} async-done(((f32[1,768,1536]{2,1,0:T(8,128)}), f32[1,96,1536]{2,1,0:T(8,128)}) %reduce-scatter.24.cloned.1.call-update) | async-done | bytes 589840 | tf_op jit(solution)/shard_map/reduce_scatter | solution.py:198
  1006.0 133.0 %reduce-scatter.14.cloned.1.call-done = f32[1,96,2304]{2,1,0:T(8,128)} async-done(((f32[1,768,2304]{2,1,0:T(8,128)}), f32[1,96,2304]{2,1,0:T(8,128)}) %reduce-scatter.14.cloned.1.call-update) | async-done | bytes 884752 | tf_op jit(solution)/shard_map/reduce_scatter | solution.py:193
  1139.1 167.1 %reduce-scatter.20.cloned.1.call-done = f32[1,384,768]{2,1,0:T(8,128)} async-done(((f32[1,3072,768]{2,1,0:T(8,128)}), f32[1,384,768]{2,1,0:T(8,128)}) %reduce-scatter.20.cloned.1.call-update) | async-done | bytes 1179664 | tf_op jit(solution)/shard_map/reduce_scatter | solution.py:196
  1306.2 167.2 %reduce-scatter.18.cloned.1.call-done = f32[1,96,3072]{2,1,0:T(8,128)} async-done(((f32[1,768,3072]{2,1,0:T(8,128)}), f32[1,96,3072]{2,1,0:T(8,128)}) %reduce-scatter.18.cloned.1.call-update) | async-done | bytes 1179664 | tf_op jit(solution)/shard_map/reduce_scatter | solution.py:195
  (248 shorter events, 209.7 us)
Async XLA Ops:
  7.2 6.6 copy-start
  7.2 642.6 %reduce-scatter.28.cloned.1.call-start = ((), (), s32[]{:S(2)}) async-start(), calls=%async_computation.16 | async-start | bytes 442368
  7.3 6.5 copy-start.3
  10.8 8.6 copy-start.25
  13.8 92.4 %copy-start.52 = (f32[768]{0:T(1024)}, f32[768]{0:T(1024)S(1)}, u32[]{:S(2)}) copy-start(f32[768]{0:T(1024)S(1)} %get-tuple-element.53) | copy-start | bytes 9220
  13.8 122.2 %copy-start.47 = (f32[768]{0:T(1024)}, f32[768]{0:T(1024)S(1)}, u32[]{:S(2)}) copy-start(f32[768]{0:T(1024)S(1)} %get-tuple-element.55) | copy-start | bytes 9220
  69.3 11.6 copy-start.20
  69.3 11.6 copy-start.12
  81.0 11.6 copy-start.23
  105.5 14.3 copy-start.8
  105.5 14.3 copy-start.38
  105.5 14.3 slice-start
  106.1 13.7 copy-start.31
  106.2 13.6 copy-start.50
  106.2 13.6 slice-start.1
  136.0 7.6 copy-start.33
  136.0 7.5 copy-start.40
  143.5 46.5 %collective-permute-start = (bf16[1296,1536]{1,0:T(8,128)(2,1)}, bf16[1296,1536]{1,0:T(8,128)(2,1)}, u32[]{:S(2)}, u32[]{:S(2)}) collective-permute-start(bf16[1296,1536]{1,0:T(8,128)(2,1)} %convolution_convert_fusion.1), channel_id=1, source_target_pairs={{0,24},{8,0},{16,8},{24,16},{1,25},{9,1},{17,9},{25,17},{2,26},{10... | collective-permute-start | bytes 11943944 | tf_op jit(solution)/shard_map/ppermute | solution.py:15
  231.6 11.6 copy-start.21
  231.6 12.9 copy-start.13
  336.1 46.1 %collective-permute-start.1 = (bf16[1296,1536]{1,0:T(8,128)(2,1)}, bf16[1296,1536]{1,0:T(8,128)(2,1)}, u32[]{:S(2)}, u32[]{:S(2)}) collective-permute-start(bf16[1296,1536]{1,0:T(8,128)(2,1)} %copy.115), channel_id=1, source_target_pairs={{0,8},{8,16},{16,24},{24,0},{1,9},{9,17},{17,25},{25,1},{2,10},{10... | collective-permute-start | bytes 11943944 | tf_op jit(solution)/shard_map/ppermute | solution.py:15
  373.6 8.6 copy-start.2
  373.6 8.6 copy-start.28
  373.6 8.6 copy-start.41
  373.6 8.6 copy-start.48
  373.6 8.6 copy-start.64
  373.7 18.7 %slice-start.2 = ((s8[4718592]{0:T(1024)(128)(4,1)}), s8[4194304]{0:T(1024)(128)(4,1)S(1)}, s32[]{:S(2)}) async-start(s8[4718592]{0:T(1024)(128)(4,1)} %bitcast.201), calls=%async_computation.20 | async-start | bytes 8388608
  377.7 11.0 copy-start.34
  377.7 14.6 slice-start.3
  392.3 18.5 %copy-start.9 = (f32[1296,768]{1,0:T(8,128)S(1)}, f32[1296,768]{1,0:T(8,128)}, u32[]{:S(2)}) copy-start(f32[1296,768]{1,0:T(8,128)} %copy-done.8) | copy-start | bytes 11943940
  392.3 18.5 %copy-start.39 = (f32[1296]{0:T(1024)S(1)}, f32[1296]{0:T(1024)}, u32[]{:S(2)}) copy-start(f32[1296]{0:T(1024)} %copy-done.38) | copy-start | bytes 15556
  392.3 18.5 %copy-start.51 = (f32[1296]{0:T(1024)S(1)}, f32[1296]{0:T(1024)}, u32[]{:S(2)}) copy-start(f32[1296]{0:T(1024)} %copy-done.50) | copy-start | bytes 15556
  392.3 18.5 %copy-start.53 = (f32[768]{0:T(1024)S(1)}, f32[768]{0:T(1024)}, u32[]{:S(2)}) copy-start(f32[768]{0:T(1024)} %copy-done.52) | copy-start | bytes 9220
  410.8 12.8 copy-start.32
  505.3 10.2 copy-start.60
  505.3 11.4 copy-start.17
  549.7 7.1 copy-start.36
  565.4 125.6 %reduce-scatter.30.cloned.1.call-start = ((), (), s32[]{:S(2)}) async-start(), calls=%async_computation.17 | async-start | bytes 442368
  570.8 192.6 %reduce-scatter.26.cloned.1.call-start = ((), (), s32[]{:S(2)}) async-start(), calls=%async_computation.15 | async-start | bytes 2654208 | tf_op jit(solution)/shard_map/reduce_scatter | solution.py:199
  576.6 258.9 %reduce-scatter.22.cloned.1.call-start = ((), (), s32[]{:S(2)}) async-start(), calls=%async_computation.13 | async-start | bytes 2654208 | tf_op jit(solution)/shard_map/reduce_scatter | solution.py:197
  582.4 325.1 %reduce-scatter.16.cloned.1.call-start = ((), (), s32[]{:S(2)}) async-start(), calls=%async_computation.10 | async-start | bytes 2654208 | tf_op jit(solution)/shard_map/reduce_scatter | solution.py:194
  588.6 417.4 %reduce-scatter.24.cloned.1.call-start = ((), (), s32[]{:S(2)}) async-start(), calls=%async_computation.14 | async-start | bytes 5308416 | tf_op jit(solution)/shard_map/reduce_scatter | solution.py:198
  597.6 541.5 %reduce-scatter.14.cloned.1.call-start = ((), (), s32[]{:S(2)}) async-start(), calls=%async_computation.9 | async-start | bytes 7962624 | tf_op jit(solution)/shard_map/reduce_scatter | solution.py:193
  609.8 696.5 %reduce-scatter.20.cloned.1.call-start = ((), (), s32[]{:S(2)}) async-start(), calls=%async_computation.12 | async-start | bytes 10616832 | tf_op jit(solution)/shard_map/reduce_scatter | solution.py:196
  626.0 847.4 %reduce-scatter.18.cloned.1.call-start = ((), (), s32[]{:S(2)}) async-start(), calls=%async_computation.11 | async-start | bytes 10616832 | tf_op jit(solution)/shard_map/reduce_scatter | solution.py:195
  640.4 6.4 copy-start.49
  640.5 6.4 copy-start.5
  640.5 6.4 copy-start.7
  (33 other events, 122.2 us)
Sparse Core Ops, SparseCore 0:
  565.5 61.7 reduce-scatter.27
  630.5 60.4 reduce-scatter.29
  695.1 68.1 reduce-scatter.25
  767.2 68.1 reduce-scatter.21
  839.4 68.0 reduce-scatter.15
  911.6 94.4 reduce-scatter.23
  1010.3 128.7 reduce-scatter.13
  1143.7 162.5 reduce-scatter.19
  1310.8 162.5 reduce-scatter.17
where the time goes:
time: 1490 us; the launch traced here: 1480 us
  waiting for transfers between devices  834 us (56%)
  matrix products  339 us (23%)
  local copies, waits for them, and re-layouts  198 us (13%)
  other arithmetic  90 us (6%)
  between operations  15.1 us (1%)
    reduce_scatter x1, waiting for transfers between devices, per_device(): lax.psum_scatter(grad_up[None], 'dp', scatter_dimension=1, tiled=True)  167 us
    reduce_scatter x1, waiting for transfers between devices, per_device(): lax.psum_scatter(grad_down[None], 'dp', scatter_dimension=1, tiled=True)  167 us
    reduce_scatter x1, waiting for transfers between devices, per_device(): lax.psum_scatter(grad_qkv[None], 'dp', scatter_dimension=1, tiled=True)  133 us
    reduce_scatter x1, waiting for transfers between devices, per_device(): lax.psum_scatter(grad_joining_keyvalue_weight[None], 'dp', scatter_dimens...  98.5 us
    reduce_scatter x1, waiting for transfers between devices, per_device(): lax.psum_scatter(grad_fq[None], 'dp', scatter_dimension=1, tiled=True)  72.1 us
    reduce_scatter x1, waiting for transfers between devices, per_device(): lax.psum_scatter(grad_out_weight[None], 'dp', scatter_dimension=1, tiled=...  72.1 us
    dot_general x7, matrix products, weight_grad(): jnp.einsum('rd,re->de', left_neighbour_view, right_neighbour_view, prefer...  69.2 us
    reduce_scatter x1, waiting for transfers between devices, per_device(): lax.psum_scatter(grad_fo[None], 'dp', scatter_dimension=1, tiled=True)  69.1 us
  transfers between devices with their start and end apart: 11, of which 10 were waited for; matrix products, arithmetic and copies ran while one was open for 11% of the time, Pallas kernels for 0%

commit v1 on v0

v1 whole, which is shorter than its diff:
```python
import functools

import jax
import jax.numpy as jnp
from jax import lax
from jax.experimental import pallas as pl
from jax.experimental.pallas import tpu as pltpu
from jax.sharding import PartitionSpec as P

HEADS = 12
HEAD = 64
SLOT = 324
CLASSES = ((112, 100), (208, 196), (336, 324))
MOST = 336
EPS = 1e-05
GELU_A = 0.7978845608028654
GELU_B = 0.044715
BF = jnp.bfloat16
F32 = jnp.float32


def dot(left, right, left_dim, right_dim):
    return lax.dot_general(
        left, right, (((left_dim,), (right_dim,)), ((), ())), preferred_element_type=F32
    )


def params(limit_mib=58):
    return pltpu.CompilerParams(vmem_limit_bytes=limit_mib * 2**20)


def cost(flops, moved):
    return pl.CostEstimate(flops=int(flops), bytes_accessed=int(moved), transcendentals=0)


def rows_of(item):
    return 112 + jnp.where(item >= 1, 96, 0) + jnp.where(item >= 2, 128, 0)


def start_of(cls_ref, clip):
    start = jnp.int32(0)
    for before in range(clip):
        start = start + rows_of(cls_ref[before])
    return pl.multiple_of(start, 16)


def start_dyn(cls_ref, clip, clips):
    start = jnp.int32(0)
    for before in range(clips):
        start = start + jnp.where(before < clip, rows_of(cls_ref[before]), 0)
    return pl.multiple_of(start, 16)


def total_of(cls_ref, clips):
    return start_of(cls_ref, clips)


def clear_tail(cls_ref, clips, refs):
    rows = refs[0].shape[0]
    total = total_of(cls_ref, clips)

    @pl.loop(0, (rows - total) // 16)
    def _(step):
        at = pl.ds(pl.multiple_of(total + step * 16, 16), 16)
        for ref in refs:
            ref[at, :] = jnp.zeros((16, ref.shape[1]), ref.dtype)


def by_class(item, body):
    for index, (rows, live) in enumerate(CLASSES):
        pl.when(item == index)(functools.partial(body, rows, live))


def norm_stats(values):
    centre = jnp.mean(values, -1, keepdims=True)
    centred = values - centre
    spread = jnp.mean(centred * centred, -1, keepdims=True)
    root = lax.rsqrt(spread + EPS)
    return centred * root, root


def norm_back(values, gain, grad, gain_acc, bias_acc):
    unit, root = norm_stats(values)
    gain_acc[...] += jnp.sum(grad * unit, 0, keepdims=True)
    bias_acc[...] += jnp.sum(grad, 0, keepdims=True)
    scaled = grad * gain
    return root * (
        scaled
        - jnp.mean(scaled, -1, keepdims=True)
        - unit * jnp.mean(scaled * unit, -1, keepdims=True)
    )


def interleave(stages, count):
    held = [dict() for _ in range(count)]
    for step in range(count + len(stages) - 1):
        for index, stage in enumerate(stages):
            if 0 <= step - index < count:
                stage(step - index, held[step - index])


def one_head(pair, head):
    lane = lax.broadcasted_iota(jnp.int32, pair.shape, 1)
    keep = lane < HEAD if head % 2 == 0 else lane >= HEAD
    return jnp.where(keep, pair, jnp.zeros_like(pair))


def pair_of(head):
    return slice(128 * (head // 2), 128 * (head // 2) + 128)


def mask_keys_lane(scores, live):
    lane = lax.broadcasted_iota(jnp.int32, scores.shape, 1)
    return jnp.where(lane < live, scores, -1e30)


def mask_keys_row(scores, live):
    head, tail = scores[:-16], scores[-16:]
    row = lax.broadcasted_iota(jnp.int32, tail.shape, 0)
    tail = jnp.where(row < live - head.shape[0], tail, -1e30)
    return jnp.concatenate([head, tail], axis=0)


def attend(load_q, load_k, load_v, store, live):
    pairs = {}

    def score(head, held):
        query = one_head(load_q(head), head) * jnp.asarray(HEAD**-0.5, BF)
        held["s"] = mask_keys_lane(dot(query, load_k(head), 1, 1), live)

    def soften(head, held):
        scores = held.pop("s")
        exps = jnp.exp(scores - jnp.max(scores, -1, keepdims=True))
        held["l"] = jnp.sum(exps, -1, keepdims=True)
        held["e"] = exps.astype(BF)

    def mix(head, held):
        mixed = dot(held.pop("e"), one_head(load_v(head), head), 1, 0) / held.pop("l")
        if head % 2 == 0:
            pairs[head // 2] = mixed
        else:
            store(head, (pairs.pop(head // 2) + mixed).astype(BF))

    interleave([score, soften, mix], HEADS)


def attend_back(load_q, load_k, load_v, load_do, load_o, store, live):
    cache = {}

    def turned(head, name, load, wide=False):
        key = (name, head // 2)
        if key not in cache:
            value = load(head).T
            cache[key] = value.astype(F32) if wide else value
        at = HEAD * (head % 2)
        return cache[key][at : at + HEAD]

    def score(head, held):
        held["q"] = one_head(load_q(head), head) * jnp.asarray(HEAD**-0.5, BF)
        held["s"] = mask_keys_row(dot(load_k(head), held["q"], 1, 1), live)
        held["do"] = one_head(load_do(head), head)
        held["dp"] = dot(load_v(head), held["do"], 1, 1)

    def soften(head, held):
        scores = held.pop("s")
        exps = jnp.exp(scores - jnp.max(scores, 0, keepdims=True))
        held["p"] = exps * (1.0 / jnp.sum(exps, 0, keepdims=True))
        held["pb"] = held["p"].astype(BF)

    def mix(head, held):
        if load_o is None:
            held["o"] = dot(turned(head, "v", load_v), held["pb"], 1, 0)
        else:
            held["o"] = turned(head, "o", load_o, True)

    def grad_score(head, held):
        row_terms = jnp.sum(held["o"] * turned(head, "do", load_do, True), 0, keepdims=True)
        held["ds"] = (held.pop("p") * (held.pop("dp") - row_terms)).astype(BF)

    def finish(head, held):
        grad = held.pop("ds")
        held["dv"] = dot(held.pop("pb"), held.pop("do"), 1, 0)
        held["dk"] = dot(grad, held.pop("q"), 1, 0)
        held["dq"] = dot(turned(head, "k", load_k), grad, 1, 0) * HEAD**-0.5
        if head % 2 == 0:
            cache["half"] = held
            return
        first = cache.pop("half")
        mixed = None
        if load_o is None:
            mixed = jnp.concatenate([first["o"], held["o"]], 0).astype(BF).T
        query = jnp.concatenate([first["dq"], held["dq"]], 0).astype(BF).T
        store(
            head,
            query,
            (first["dk"] + held["dk"]).astype(BF),
            (first["dv"] + held["dv"]).astype(BF),
            mixed,
        )

    interleave([score, soften, mix, grad_score, finish], HEADS)


def pack_clip(cls_ref, clip, source, target, masked):
    start = start_of(cls_ref, clip)

    def copy(rows, live):
        held = min(rows, SLOT)
        value = source[clip * SLOT : clip * SLOT + held, :]
        if masked:
            row = lax.broadcasted_iota(jnp.int32, value.shape, 0)
            value = jnp.where(row < live, value, jnp.zeros_like(value))
        if rows > held:
            pad = jnp.zeros((rows - held, value.shape[1]), value.dtype)
            value = jnp.concatenate([value, pad], 0)
        target[pl.ds(start, rows), :] = value

    by_class(cls_ref[clip], copy)


def whole(shape):
    zeros = (0,) * len(shape)
    return pl.BlockSpec(shape, lambda *_: zeros, pipeline_mode=pl.Buffered(1))


def whole_out(shape):
    zeros = (0,) * len(shape)
    return pl.BlockSpec(shape, lambda *_: zeros)


def tile(rows, columns):
    return pl.BlockSpec((rows, columns), lambda i, *_: (i, 0))


def pack_rows(cotangent, classes, rows):
    clips = classes.shape[0]
    width = cotangent.shape[1]

    def kernel(cls_ref, source, target):
        for clip in range(clips):
            pack_clip(cls_ref, clip, source, target, True)
        clear_tail(cls_ref, clips, [target])

    return pl.pallas_call(
        kernel,
        grid_spec=pltpu.PrefetchScalarGridSpec(
            num_scalar_prefetch=1,
            grid=(1,),
            in_specs=[whole(cotangent.shape)],
            out_specs=whole_out((rows, width)),
        ),
        out_shape=jax.ShapeDtypeStruct((rows, width), BF),
        compiler_params=params(),
        cost_estimate=cost(0, 4 * rows * width),
    )(classes, cotangent)


def norm_project(tokens, classes, rows, gain, bias, weight, step):
    clips = classes.shape[0]
    width, wide = weight.shape

    def kernel(cls_ref, tok_ref, gain_ref, bias_ref, w_ref, x_ref, h_ref, qkv_ref):
        index = pl.program_id(0)

        @pl.when(index == 0)
        def _():
            for clip in range(clips):
                pack_clip(cls_ref, clip, tok_ref, x_ref, False)
            clear_tail(cls_ref, clips, [x_ref])

        live = index * step < total_of(cls_ref, clips)

        @pl.when(live)
        def _():
            at = pl.ds(pl.multiple_of(index * step, 16), step)
            unit, _ = norm_stats(x_ref[at, :].astype(F32))
            low = (unit * gain_ref[...] + bias_ref[...]).astype(BF)
            h_ref[...] = low
            qkv_ref[...] = dot(low, w_ref[...], 1, 0).astype(BF)

        @pl.when(jnp.logical_not(live))
        def _():
            h_ref[...] = jnp.zeros_like(h_ref)
            qkv_ref[...] = jnp.zeros_like(qkv_ref)

    return pl.pallas_call(
        kernel,
        grid_spec=pltpu.PrefetchScalarGridSpec(
            num_scalar_prefetch=1,
            grid=(rows // step,),
            in_specs=[whole(tokens.shape), whole(gain.shape), whole(bias.shape), whole(weight.shape)],
            out_specs=[whole_out((rows, width)), tile(step, width), tile(step, wide)],
        ),
        out_shape=[
            jax.ShapeDtypeStruct((rows, width), BF),
            jax.ShapeDtypeStruct((rows, width), BF),
            jax.ShapeDtypeStruct((rows, wide), BF),
        ],
        compiler_params=params(),
        cost_estimate=cost(2 * rows * width * wide, 2 * rows * (3 * width + wide) + 2 * weight.size),
    )(classes, tokens, gain, bias, weight)


def self_attend(qkv, classes):
    clips = classes.shape[0]
    rows, wide = qkv.shape
    width = wide // 3

    def kernel(cls_ref, qkv_ref, o_ref):
        clip = pl.program_id(0)
        start = start_dyn(cls_ref, clip, clips)

        def body(count, live):
            at = pl.ds(start, count)

            def load(part):
                def get(head):
                    pair = pair_of(head)
                    return qkv_ref[at, part * width + pair.start : part * width + pair.stop]

                return get

            def store(head, mixed):
                o_ref[at, pair_of(head)] = mixed

            attend(load(0), load(1), load(2), store, live)

        by_class(cls_ref[clip], body)

        @pl.when(clip == clips - 1)
        def _():
            clear_tail(cls_ref, clips, [o_ref])

    return pl.pallas_call(
        kernel,
        grid_spec=pltpu.PrefetchScalarGridSpec(
            num_scalar_prefetch=1,
            grid=(clips,),
            in_specs=[whole(qkv.shape)],
            out_specs=whole_out((rows, width)),
        ),
        out_shape=jax.ShapeDtypeStruct((rows, width), BF),
        compiler_params=params(),
        cost_estimate=cost(16 * rows * MOST * width, 2 * rows * (wide + width)),
    )(classes, qkv)


def feed_forward(x, mixed, classes, gains, biases, w_out, w_up, w_down, w_fq, step):
    clips = classes.shape[0]
    rows, width = x.shape
    hidden = w_up.shape[1]
    chunk = width

    def kernel(
        cls_ref, x_ref, o_ref, gain_ref, bias_ref, out_w, up_w, down_w, fq_w,
        mid_ref, h_ref, u_ref, act_ref, layer_ref, n_ref, fq_ref,
    ):
        live = pl.program_id(0) * step < total_of(cls_ref, clips)

        @pl.when(live)
        def _():
            middle = x_ref[...].astype(F32) + dot(o_ref[...], out_w[...], 1, 0)
            mid_ref[...] = middle
            unit, _ = norm_stats(middle)
            low = (unit * gain_ref[1:2] + bias_ref[1:2]).astype(BF)
            h_ref[...] = low
            layer = middle
            for at in range(0, hidden, chunk):
                part = slice(at, at + chunk)
                up = dot(low, up_w[:, part], 1, 0)
                inner = jnp.tanh(GELU_A * (up + GELU_B * (up * up * up)))
                act = (0.5 * up * (1.0 + inner)).astype(BF)
                u_ref[:, part] = up.astype(BF)
                act_ref[:, part] = act
                layer = layer + dot(act, down_w[part, :], 1, 0)
            layer_ref[...] = layer
            unit, _ = norm_stats(layer)
            low = (unit * gain_ref[2:3] + bias_ref[2:3]).astype(BF)
            n_ref[...] = low
            fq_ref[...] = dot(low, fq_w[...], 1, 0).astype(BF)

        @pl.when(jnp.logical_not(live))
        def _():
            for ref in (mid_ref, h_ref, u_ref, act_ref, layer_ref, n_ref, fq_ref):
                ref[...] = jnp.zeros_like(ref)

    shapes = [(width, F32), (width, BF), (hidden, BF), (hidden, BF), (width, F32), (width, BF), (width, BF)]
    weights = [w_out, w_up, w_down, w_fq]
    return pl.pallas_call(
        kernel,
        grid_spec=pltpu.PrefetchScalarGridSpec(
            num_scalar_prefetch=1,
            grid=(rows // step,),
            in_specs=[tile(step, width), tile(step, width), whole(gains.shape), whole(biases.shape)]
            + [whole(w.shape) for w in weights],
            out_specs=[tile(step, columns) for columns, _ in shapes],
        ),
        out_shape=[jax.ShapeDtypeStruct((rows, columns), kind) for columns, kind in shapes],
        compiler_params=params(),
        cost_estimate=cost(
            2 * rows * sum(w.size for w in weights),
            2 * sum(w.size for w in weights) + rows * (4 * 5 * width + 4 * hidden),
        ),
    )(classes, x, mixed, gains, biases, *weights)


def join_attend(arrived, fq, grad, w_kv, w_out, classes):
    clips = classes.shape[0]
    rows, width = fq.shape
    wide = w_kv.shape[1]

    def kernel(cls_ref, n_ref, q_ref, g_ref, kv_w, out_w, o_ref, dq_ref, dkv_ref, dn_ref, kv, do):
        clip = pl.program_id(0)
        start = start_dyn(cls_ref, clip, clips)

        def body(count, live):
            at = pl.ds(start, count)
            kv[:count, :] = dot(n_ref[at, :], kv_w[...], 1, 0).astype(BF)
            do[:count, :] = dot(g_ref[at, :], out_w[...], 1, 1).astype(BF)

            def load_q(head):
                return q_ref[at, pair_of(head)]

            def load_k(head):
                return kv[:count, pair_of(head)]

            def load_v(head):
                pair = pair_of(head)
                return kv[:count, width + pair.start : width + pair.stop]

            def load_do(head):
                return do[:count, pair_of(head)]

            def store(head, query, key, value, mixed):
                pair = pair_of(head)
                o_ref[at, pair] = mixed
                dq_ref[at, pair] = query
                dkv_ref[at, pair] = key
                dkv_ref[at, width + pair.start : width + pair.stop] = value

            attend_back(load_q, load_k, load_v, load_do, None, store, live)
            dn_ref[at, :] = dot(dkv_ref[at, :], kv_w[...], 1, 1).astype(BF)

        by_class(cls_ref[clip], body)

        @pl.when(clip == clips - 1)
        def _():
            clear_tail(cls_ref, clips, [o_ref, dq_ref, dkv_ref, dn_ref])

    outs = [width, width, wide, width]
    return pl.pallas_call(
        kernel,
        grid_spec=pltpu.PrefetchScalarGridSpec(
            num_scalar_prefetch=1,
            grid=(clips,),
            in_specs=[whole(v.shape) for v in (arrived, fq, grad, w_kv, w_out)],
            out_specs=[whole_out((rows, columns)) for columns in outs],
            scratch_shapes=[pltpu.VMEM((MOST, wide), BF), pltpu.VMEM((MOST, width), BF)],
        ),
        out_shape=[jax.ShapeDtypeStruct((rows, columns), BF) for columns in outs],
        compiler_params=params(),
        cost_estimate=cost(64 * rows * MOST * width, 20 * rows * width),
    )(classes, arrived, fq, grad, w_kv, w_out)


def join_result(layer, mixed, w_out, classes, slots):
    clips = classes.shape[0]
    rows, width = layer.shape

    def kernel(cls_ref, layer_ref, o_ref, w_ref, out_ref):
        for clip in range(clips):
            start = start_of(cls_ref, clip)

            def body(count, live):
                at = pl.ds(start, count)
                value = layer_ref[at, :] + dot(o_ref[at, :], w_ref[...], 1, 0)
                held = min(count, SLOT)
                row = lax.broadcasted_iota(jnp.int32, value.shape, 0)
                value = jnp.where(row < live, value, 0.0).astype(BF)
                first = clip * SLOT
                out_ref[first : first + held, :] = value[:held]
                if held < SLOT:
                    out_ref[first + held : first + SLOT, :] = jnp.zeros((SLOT - held, width), BF)

            by_class(cls_ref[clip], body)

    return pl.pallas_call(
        kernel,
        grid_spec=pltpu.PrefetchScalarGridSpec(
            num_scalar_prefetch=1,
            grid=(1,),
            in_specs=[whole(v.shape) for v in (layer, mixed, w_out)],
            out_specs=whole_out((slots, width)),
        ),
        out_shape=jax.ShapeDtypeStruct((slots, width), BF),
        compiler_params=params(),
        cost_estimate=cost(2 * rows * width * width, 8 * rows * width + 2 * w_out.size),
    )(classes, layer, mixed, w_out)


def feed_forward_back(dfq, back, layer, grad, up, middle, classes, gains, w_fq, w_down, w_up, w_out, step):
    clips = classes.shape[0]
    rows, width = layer.shape
    hidden = w_up.shape[1]
    chunk = width

    def kernel(
        cls_ref, dfq_ref, back_ref, layer_ref, g_ref, u_ref, mid_ref, gain_ref, fq_w, down_w, up_w, out_w,
        down_ref, hid_ref, gmid_ref, low_ref, do_ref, gain_three, bias_three, gain_two, bias_two,
    ):
        @pl.when(pl.program_id(0) == 0)
        def _():
            for ref in (gain_three, bias_three, gain_two, bias_two):
                ref[...] = jnp.zeros_like(ref)

        live = pl.program_id(0) * step < total_of(cls_ref, clips)

        @pl.when(live)
        def _():
            grad_norm = dot(dfq_ref[...], fq_w[...], 1, 1) + back_ref[...].astype(F32)
            grad_layer = g_ref[...].astype(F32) + norm_back(
                layer_ref[...], gain_ref[2:3], grad_norm, gain_three, bias_three
            )
            down_low = grad_layer.astype(BF)
            down_ref[...] = down_low
            grad_norm = jnp.zeros((step, width), F32)
            for at in range(0, hidden, chunk):
                part = slice(at, at + chunk)
                grad_act = dot(down_low, down_w[part, :], 1, 1)
                value = u_ref[:, part].astype(F32)
                square = value * value
                inner = jnp.tanh(GELU_A * (value + GELU_B * (square * value)))
                slope = 0.5 * (1.0 + inner) + (0.5 * GELU_A) * value * (1.0 - inner * inner) * (
                    1.0 + (3.0 * GELU_B) * square
                )
                low = (grad_act * slope).astype(BF)
                hid_ref[:, part] = low
                grad_norm = grad_norm + dot(low, up_w[:, part], 1, 1)
            grad_middle = grad_layer + norm_back(
                mid_ref[...], gain_ref[1:2], grad_norm, gain_two, bias_two
            )
            gmid_ref[...] = grad_middle
            low = grad_middle.astype(BF)
            low_ref[...] = low
            do_ref[...] = dot(low, out_w[...], 1, 1).astype(BF)

        @pl.when(jnp.logical_not(live))
        def _():
            for ref in (down_ref, hid_ref, gmid_ref, low_ref, do_ref):
                ref[...] = jnp.zeros_like(ref)

    shapes = [(width, BF), (hidden, BF), (width, F32), (width, BF), (width, BF)]
    weights = [w_fq, w_down, w_up, w_out]
    return pl.pallas_call(
        kernel,
        grid_spec=pltpu.PrefetchScalarGridSpec(
            num_scalar_prefetch=1,
            grid=(rows // step,),
            in_specs=[
                tile(step, width), tile(step, width), tile(step, width), tile(step, width),
                tile(step, hidden), tile(step, width), whole(gains.shape),
            ]
            + [whole(w.shape) for w in weights],
            out_specs=[tile(step, columns) for columns, _ in shapes] + [whole_out((1, width))] * 4,
        ),
        out_shape=[jax.ShapeDtypeStruct((rows, columns), kind) for columns, kind in shapes]
        + [jax.ShapeDtypeStruct((1, width), F32)] * 4,
        compiler_params=params(),
        cost_estimate=cost(
            2 * rows * sum(w.size for w in weights),
            2 * sum(w.size for w in weights) + rows * (4 * 7 * width + 4 * hidden),
        ),
    )(classes, dfq, back, layer, grad, up, middle, gains, *weights)


def self_attend_back(qkv, mixed, grad, classes):
    clips = classes.shape[0]
    rows, wide = qkv.shape
    width = wide // 3

    def kernel(cls_ref, qkv_ref, o_ref, do_ref, d_ref):
        clip = pl.program_id(0)
        start = start_dyn(cls_ref, clip, clips)

        def body(count, live):
            at = pl.ds(start, count)

            def columns(part, head):
                pair = pair_of(head)
                return slice(part * width + pair.start, part * width + pair.stop)

            def load(part):
                return lambda head: qkv_ref[at, columns(part, head)]

            def store(head, query, key, value, _):
                for part, result in enumerate((query, key, value)):
                    d_ref[at, columns(part, head)] = result

            attend_back(
                load(0),
                load(1),
                load(2),
                lambda head: do_ref[at, pair_of(head)],
                lambda head: o_ref[at, pair_of(head)],
                store,
                live,
            )

        by_class(cls_ref[clip], body)

        @pl.when(clip == clips - 1)
        def _():
            clear_tail(cls_ref, clips, [d_ref])

    return pl.pallas_call(
        kernel,
        grid_spec=pltpu.PrefetchScalarGridSpec(
            num_scalar_prefetch=1,
            grid=(clips,),
            in_specs=[whole(v.shape) for v in (qkv, mixed, grad)],
            out_specs=whole_out((rows, wide)),
        ),
        out_shape=jax.ShapeDtypeStruct((rows, wide), BF),
        compiler_params=params(),
        cost_estimate=cost(48 * rows * MOST * width, 16 * rows * width),
    )(classes, qkv, mixed, grad)


def norm_project_back(dqkv, x, gmid, classes, gain, weight, step, slots):
    clips = classes.shape[0]
    rows, width = x.shape
    wide = weight.shape[1]

    def kernel(cls_ref, d_ref, x_ref, gmid_ref, gain_ref, w_ref, out_ref, gain_one, bias_one, packed):
        index = pl.program_id(0)

        @pl.when(index == 0)
        def _():
            gain_one[...] = jnp.zeros_like(gain_one)
            bias_one[...] = jnp.zeros_like(bias_one)

        @pl.when(index * step < total_of(cls_ref, clips))
        def _():
            grad_norm = dot(d_ref[...], w_ref[...], 1, 1)
            at = pl.ds(pl.multiple_of(index * step, 16), step)
            packed[at, :] = gmid_ref[...] + norm_back(
                x_ref[...].astype(F32), gain_ref[...], grad_norm, gain_one, bias_one
            )

        @pl.when(index == rows // step - 1)
        def _():
            for clip in range(clips):
                start = start_of(cls_ref, clip)

                def body(count, live):
                    value = packed[pl.ds(start, count), :]
                    held = min(count, SLOT)
                    first = clip * SLOT
                    out_ref[first : first + held, :] = value[:held]
                    if held < SLOT:
                        out_ref[first + held : first + SLOT, :] = jnp.zeros((SLOT - held, width), F32)

                by_class(cls_ref[clip], body)

    return pl.pallas_call(
        kernel,
        grid_spec=pltpu.PrefetchScalarGridSpec(
            num_scalar_prefetch=1,
            grid=(rows // step,),
            in_specs=[
                tile(step, wide), tile(step, width), tile(step, width), whole(gain.shape), whole(weight.shape),
            ],
            out_specs=[whole_out((slots, width))] + [whole_out((1, width))] * 2,
            scratch_shapes=[pltpu.VMEM((rows, width), F32)],
        ),
        out_shape=[jax.ShapeDtypeStruct((slots, width), F32)] + [jax.ShapeDtypeStruct((1, width), F32)] * 2,
        compiler_params=params(),
        cost_estimate=cost(2 * rows * width * wide, rows * (10 * width + 2 * wide) + 2 * weight.size),
    )(classes, dqkv, x, gmid, gain, weight)


def bits_of(count):
    return count.bit_length() - 1


def place_to_part(place, order):
    part = 0
    for index, bit in enumerate(order):
        if place >> (len(order) - 1 - index) & 1:
            part |= 1 << bit
    return part


def weight_grads(own, products, shards, order):
    width = products[0][0].shape[1]
    rows = products[0][0].shape[0]
    blocks = [right.shape[1] // width for _, right in products]
    total = sum(blocks)
    part_rows = width // shards
    half = shards // 2

    def kernel(own_ref, *refs):
        lefts = refs[: len(products)]
        rights = refs[len(products) : 2 * len(products)]
        kept, sent, acc = refs[2 * len(products) :]
        index = pl.program_id(0)
        first = 0
        for left, right, count in zip(lefts, rights, blocks):

            @pl.when((index >= first) & (index < first + count))
            def _():
                acc[...] = dot(left[...], right[...], 0, 0)

            first += count
        for place in range(shards):
            owner = own_ref[0] ^ place_to_part(place, order)
            part = acc[pl.ds(pl.multiple_of(owner * part_rows, 8), part_rows), :].astype(BF)
            if place < half:
                kept[place] = part
            else:
                sent[place - half] = part

    def right_spec(first, count):
        return pl.BlockSpec((rows, width), lambda j, *_: (0, jnp.clip(j - first, 0, count - 1)))

    firsts = [sum(blocks[:i]) for i in range(len(blocks))]
    out = pl.BlockSpec((half, part_rows, width), lambda j, *_: (0, 0, j))
    return pl.pallas_call(
        kernel,
        grid_spec=pltpu.PrefetchScalarGridSpec(
            num_scalar_prefetch=1,
            grid=(total,),
            in_specs=[whole(left.shape) for left, _ in products]
            + [right_spec(first, count) for first, count in zip(firsts, blocks)],
            out_specs=[out, out],
            scratch_shapes=[pltpu.VMEM((width, width), F32)],
        ),
        out_shape=[jax.ShapeDtypeStruct((half, part_rows, width * total), BF)] * 2,
        compiler_params=params(),
        cost_estimate=cost(
            2 * rows * width * width * total,
            2 * rows * width * (len(products) + total) + 2 * width * width * total,
        ),
    )(own, *[left for left, _ in products], *[right for _, right in products])


def weight_grads_tall(own, left, right, shards, order):
    rows, tall = left.shape
    width = right.shape[1]
    part_rows = tall // shards
    half = shards // 2
    blocks = tall // width
    per_block = width // part_rows

    def kernel(own_ref, left_ref, right_ref, kept, sent, acc):
        index = pl.program_id(0)
        acc[...] = dot(left_ref[...], right_ref[...], 0, 0)
        for sub in range(per_block):
            part = acc[sub * part_rows : (sub + 1) * part_rows, :].astype(BF)
            distance = own_ref[0] ^ (index * per_block + sub)
            place = jnp.int32(0)
            for position, bit in enumerate(order):
                place = place | (((distance >> bit) & 1) << (len(order) - 1 - position))

            @pl.when(place < half)
            def _():
                kept[jnp.minimum(place, half - 1)] = part

            @pl.when(place >= half)
            def _():
                sent[jnp.maximum(place - half, 0)] = part

    return pl.pallas_call(
        kernel,
        grid_spec=pltpu.PrefetchScalarGridSpec(
            num_scalar_prefetch=1,
            grid=(blocks,),
            in_specs=[pl.BlockSpec((rows, width), lambda j, *_: (0, j)), whole(right.shape)],
            out_specs=[whole_out((half, part_rows, width))] * 2,
            scratch_shapes=[pltpu.VMEM((width, width), F32)],
        ),
        out_shape=[jax.ShapeDtypeStruct((half, part_rows, width), BF)] * 2,
        compiler_params=params(),
        cost_estimate=cost(2 * rows * tall * width, 2 * rows * (tall + width) + 2 * tall * width),
    )(own, left, right)


def exchange(value, bit):
    count = lax.axis_size("dp")
    return lax.ppermute(value, "dp", [(i, i ^ (1 << bit)) for i in range(count)])


def halve(kept, sent, order):
    for index, bit in enumerate(order):
        got = exchange(sent, bit)
        value = kept.astype(F32) + got.astype(F32)
        if index == len(order) - 1:
            return value[0]
        low = value.astype(BF)
        half = low.shape[0] // 2
        kept, sent = low[:half], low[half:]


def shifted(value, axis, steps):
    count = lax.axis_size(axis)
    return lax.ppermute(value, axis, [(source, (source + steps) % count) for source in range(count)])


def per_device(
    tokens, item_class, norm_gain, norm_bias, attn_qkv, attn_out, mlp_up, mlp_down,
    join_query, join_keyval, join_output, cotangent,
):
    width = tokens.shape[2]
    slots = tokens.shape[1]
    clips = item_class.shape[0]
    rows = clips * MOST
    shards = lax.axis_size("dp")
    step = MOST
    gains, biases = norm_gain[0], norm_bias[0]
    w_qkv, w_out, w_up, w_down = attn_qkv[0], attn_out[0], mlp_up[0], mlp_down[0]
    w_fq, w_fkv, w_fo = join_query[0], join_keyval[0], join_output[0]
    own = lax.axis_index("dp").astype(jnp.int32)[None]

    next_fkv = shifted(w_fkv, "view", -1)
    x, low_one, qkv = norm_project(tokens[0], item_class, rows, gains[:1], biases[:1], w_qkv, step)
    mixed = self_attend(qkv, item_class)
    middle, low_two, up, act, layer, low_three, fq = feed_forward(
        x, mixed, item_class, gains, biases, w_out, w_up, w_down, w_fq, step
    )
    arrived = shifted(low_three, "view", -1)
    grad = pack_rows(cotangent[0], item_class, rows)
    join_mixed, dfq, dkv, back = join_attend(arrived, fq, grad, next_fkv, w_fo, item_class)
    returned = shifted(back, "view", 1)
    joined = join_result(layer, join_mixed, w_fo, item_class, slots)

    order = (0, 1, 2)
    sum_join = halve(
        *weight_grads(own, [(join_mixed, grad), (low_three, dfq), (arrived, dkv)], shards, order), order
    )
    down_low, hidden_low, gmid, out_low, do_self, gain_three, bias_three, gain_two, bias_two = feed_forward_back(
        dfq, returned, layer, grad, up, middle, item_class, gains, w_fq, w_down, w_up, w_out, step
    )
    sum_down = halve(*weight_grads_tall(own, act, down_low, shards, order), order)
    sum_up = halve(*weight_grads(own, [(low_two, hidden_low)], shards, order), order)
    dqkv = self_attend_back(qkv, mixed, do_self, item_class)
    sum_self = halve(*weight_grads(own, [(mixed, out_low), (low_one, dqkv)], shards, order), order)
    grad_tokens, gain_one, bias_one = norm_project_back(
        dqkv, x, gmid, item_class, gains[:1], w_qkv, step, slots
    )
    small = jnp.concatenate([gain_one, gain_two, gain_three, bias_one, bias_two, bias_three], 0)
    small = lax.psum_scatter(small, "dp", scatter_dimension=1, tiled=True)
    sum_fkv = shifted(sum_join[:, 2 * width :], "view", 1)
    return (
        joined[None],
        grad_tokens[None],
        small[None, :3],
        small[None, 3:],
        sum_self[None, :, width:],
        sum_self[None, :, :width],
        sum_up[None],
        sum_down[None],
        sum_join[None, :, width : 2 * width],
        sum_fkv[None],
        sum_join[None, :, :width],
    )


def solution(mesh):
    weight = P("view", None, None)
    tokens = P("view", "dp", None)
    small = P("view", None, "dp")
    return jax.shard_map(
        per_device,
        mesh=mesh,
        in_specs=(tokens, P("dp")) + (weight,) * 9 + (tokens,),
        out_specs=(tokens, tokens, small, small) + (tokens,) * 7,
        check_vma=False,
    )
```

time: 1490 us -> 520 us (0.35)
  waiting for transfers between devices: 834 us -> 207 us
  matrix products: 339 us -> 0 us
  Pallas kernels: 0 us -> 195 us
  local copies, waits for them, and re-layouts: 198 us -> 21.1 us
  other arithmetic: 90 us -> 15.5 us
  starting transfers between devices: 3.64 us -> 62.2 us
    reduce_scatter x7 -> x0, waiting for transfers between devices: 779 us -> none  [the longest x1 167 us: per_device(): lax.psum_scatter(grad_up[None], 'dp', scatter_dimension=1, tiled=True)]
    dot_general x33 -> x0, matrix products: 339 us -> none  [the longest x7 69.2 us: weight_grad(): jnp.einsum('rd,re->de', left_neighbour_view, right_neighbour_view, prefer...]
    pallas_call x0 -> x13, Pallas kernels: none -> 195 us  [the longest x3 40.1 us: weight_grads(): pl.pallas_call(kernel, grid_spec=pltpu.PrefetchScalarGridSpec(num_scalar_...]
    ppermute x2 -> x16, waiting for transfers between devices: 16.3 us -> 140 us  [the longest x12 118 us: exchange(): return lax.ppermute(value, 'dp', [(i, i ^ 1 << bit) for i in range(count)])]
    reshape x19 -> x0, local copies, waits for them, and re-layouts: 76 us -> none  [the longest x8 47.7 us: reshape_into_heads(): return rows.reshape(count, SLOT, HEADS, rows.shape[1] // HEADS)]
    ppermute x2 -> x16, starting transfers between devices: 3.27 us -> 62.2 us  [the longest x12 58.7 us: exchange(): return lax.ppermute(value, 'dp', [(i, i ^ 1 << bit) for i in range(count)])]
    convert_element_type x10 -> x0, local copies, waits for them, and re-layouts: 38.3 us -> none  [the longest x2 8.54 us: per_device(): grad_fq_low = grad_fq_rows.astype(jnp.bfloat16)]
    reduce_sum x9 -> x0, other arithmetic: 34.3 us -> none  [the longest x2 23.2 us: attend(): totals = jnp.sum(exp_scores, -1, keepdims=True)]
  transfers between devices with their start and end apart: 11 -> 17, of which waited for: 10 -> 8; matrix products, arithmetic and copies ran while one was open for 11% -> 6% of each run, Pallas kernels for 0% -> 33%
where the time goes in v1:
time: 520 us; the launch traced here: 515 us
  waiting for transfers between devices  207 us (40%)
  Pallas kernels  195 us (38%)
  starting transfers between devices  62.2 us (12%)
  local copies, waits for them, and re-layouts  21.1 us (4%)
  other arithmetic  15.5 us (3%)
  between operations  14.5 us (3%)
    ppermute x12, waiting for transfers between devices, exchange(): return lax.ppermute(value, 'dp', [(i, i ^ 1 << bit) for i in range(count)])  118 us
    unnamed x2, waiting for transfers between devices  66.1 us
    ppermute x12, starting transfers between devices, exchange(): return lax.ppermute(value, 'dp', [(i, i ^ 1 << bit) for i in range(count)])  58.7 us
    pallas_call x3, Pallas kernels, weight_grads(): pl.pallas_call(kernel, grid_spec=pltpu.PrefetchScalarGridSpec(num_scalar_...  40.1 us
    pallas_call x1, Pallas kernels, feed_forward_back(): pl.pallas_call(kernel, grid_spec=pltpu.PrefetchScalarGridSpec(num_scalar_...  30.4 us
    pallas_call x1, Pallas kernels, feed_forward(): pl.pallas_call(kernel, grid_spec=pltpu.PrefetchScalarGridSpec(num_scalar_...  27 us
    pallas_call x1, Pallas kernels, join_attend(): pl.pallas_call(kernel, grid_spec=pltpu.PrefetchScalarGridSpec(num_scalar_...  25.5 us
    ppermute x4, waiting for transfers between devices, shifted(): lax.ppermute(value, axis, [(source, (source + steps) % count) for source...  22.4 us
  transfers between devices with their start and end apart: 17, of which 8 were waited for; matrix products, arithmetic and copies ran while one was open for 6% of the time, Pallas kernels for 33%

profile of v1, /device:TPU:0, one launch (start us, length us, event | category | flops | bytes accessed | tf_op | source)
XLA Modules:
  0.0 514.7 jit_solution(8476876752888128175)
XLA Ops:
  7.2 2.4 collective-permute-start.1
  9.7 1.3 copy.36
  11.0 1.3 slice_bitcast_fusion.4
  12.2 1.3 copy.35
  13.5 11.4 %shard_map.203 = (bf16[1344,768]{1,0:T(8,128)(2,1)}, bf16[1344,768]{1,0:T(8,128)(2,1)}, bf16[1344,2304]{1,0:T(8,128)(2,1)}) custom-call(s32[4]{0:T(128)} %cls_ref.17, bf16[1296,768]{1,0:T(8,128)(2,1)} %bitcast.58, f32[1,768]{1,0:T(1,128)} %get-tuple-element.106.gain_ref, f32[1,768]{1,0:T(1,128)} %get-tuple-element.105.bias_ref, bf16[768,2304]{1,0:T(8,128)(2,1)} %bitcast.55), custom_call_target="tpu_custom_call" | custom-call | flops 4756340736 | bytes 15925248 | tf_op jit(solution)/shard_map/pallas_call | solution.py:286
  24.9 9.4 %shard_map.204.o_ref.refs_0_ = bf16[1344,768]{1,0:T(8,128)(2,1)} custom-call(s32[4]{0:T(128)} %cls_ref.17, bf16[1344,2304]{1,0:T(8,128)(2,1)} %get-tuple-element.46.qkv_ref), custom_call_target="tpu_custom_call" | custom-call | flops 5549064192 | bytes 8257536 | tf_op jit(solution)/shard_map/pallas_call | solution.py:334
  34.4 27.0 %shard_map.205 = (f32[1344,768]{1,0:T(8,128)}, bf16[1344,768]{1,0:T(8,128)(2,1)}, bf16[1344,3072]{1,0:T(8,128)(2,1)}, bf16[1344,3072]{1,0:T(8,128)(2,1)}, f32[13...) custom-call(s32[4]{0:T(128)} %cls_ref.17, bf16[1344,768]{1,0:T(8,128)(2,1)} %get-tuple-element.45.x_ref, ...), custom_call_target="tpu_custom_call" | custom-call | flops 15854469120 | bytes 48955392 | tf_op jit(solution)/shard_map/pallas_call | solution.py:389
  62.1 3.9 shard_map.206.g_ref.refs_3_
  66.0 19.6 %collective-permute-done.n_ref.refs_2_ = bf16[1344,768]{1,0:T(8,128)(2,1)S(1)} collective-permute-done((bf16[1344,768]{1,0:T(8,128)(2,1)}, bf16[1344,768]{1,0:T(8,128)(2,1)S(1)}, u32[]{:S(2)}, u32[]{:S(2)}) %collective-permute-start) | collective-permute-done | bytes 2064416 | tf_op jit(solution)/shard_map/ppermute | solution.py:806
  85.6 1.3 copy-done.10
  87.7 25.5 %shard_map.207 = (bf16[1344,768]{1,0:T(8,128)(2,1)}, bf16[1344,768]{1,0:T(8,128)(2,1)}, bf16[1344,1536]{1,0:T(8,128)(2,1)}, bf16[1344,768]{1,0:T(8,128)(2,1)}) custom-call(s32[4]{0:T(128)} %cls_ref.17, bf16[1344,768]{1,0:T(8,128)(2,1)} %copy-done.10, bf16[1344,768]{1,0:T(8,128)(2,1)} %get-tuple-element.49.q_ref, bf16[1344,768]{1,0:T(8,128)(2,1)} %shard_map.206.g_ref.refs_3_, ...), custom_call_target="tpu_custom_call" | custom-call | flops 22196256768 | bytes 20643840 | tf_op jit(solution)/shard_map/pallas_call | solution.py:451
  113.3 14.5 %shard_map.215 = (bf16[4,96,3072]{2,1,0:T(8,128)(2,1)}, bf16[4,96,3072]{2,1,0:T(8,128)(2,1)}) custom-call(s32[1]{0:T(128)} %bitcast.17.own_ref, bf16[1344,768]{1,0:T(8,128)(2,1)} %get-tuple-element.50.o_ref.refs_0_, bf16[1344,768]{1,0:T(8,128)(2,1)} %get-tuple-element.48.refs_1_, bf16[1344,768]{1,0:T(8,128)(2,1)} %copy-done.10, ...), custom_call_target="tpu_custom_call" | custom-call | flops 6341787648 | bytes 19169280 | tf_op jit(solution)/shard_map/pallas_call | solution.py:728
  127.8 8.0 %collective-permute-start.12 = (bf16[4,96,3072]{2,1,0:T(8,128)(2,1)}, bf16[4,96,3072]{2,1,0:T(8,128)(2,1)S(1)}, u32[]{:S(2)}, u32[]{:S(2)}) collective-permute-start(bf16[4,96,3072]{2,1,0:T(8,128)(2,1)} %get-tuple-element.78), channel_id=1, source_target_pairs={{0,1},{1,0},{2,3},{3,2},{4,5},{5,4},{6,7},{7,6},{8,9},{9,8},{10,11... | collective-permute-start | bytes 7077896 | tf_op jit(solution)/shard_map/ppermute | solution.py:790
  135.8 2.8 collective-permute-done.2.back_ref
  138.6 1.3 copy-done.9
  139.9 30.4 %shard_map.209 = (bf16[1344,768]{1,0:T(8,128)(2,1)}, bf16[1344,3072]{1,0:T(8,128)(2,1)}, f32[1344,768]{1,0:T(8,128)}, bf16[1344,768]{1,0:T(8,128)(2,1)}, bf16[13...) custom-call(s32[4]{0:T(128)} %cls_ref.17, ...), custom_call_target="tpu_custom_call" | custom-call | flops 15854469120 | bytes 57212928 | tf_op jit(solution)/shard_map/pallas_call | solution.py:554
  170.3 13.1 %shard_map.214 = (bf16[4,384,768]{2,1,0:T(8,128)(2,1)}, bf16[4,384,768]{2,1,0:T(8,128)(2,1)}) custom-call(s32[1]{0:T(128)} %bitcast.17.own_ref, bf16[1344,3072]{1,0:T(8,128)(2,1)} %get-tuple-element.72.left_ref, bf16[1344,768]{1,0:T(8,128)(2,1)} %get-tuple-element.73.right_ref), custom_call_target="tpu_custom_call" | custom-call | flops 6341787648 | bytes 15040512 | tf_op jit(solution)/shard_map/pallas_call | solution.py:773
  183.5 7.4 %collective-permute-start.9 = (bf16[4,384,768]{2,1,0:T(8,128)(2,1)}, bf16[4,384,768]{2,1,0:T(8,128)(2,1)}, u32[]{:S(2)}, u32[]{:S(2)}) collective-permute-start(bf16[4,384,768]{2,1,0:T(8,128)(2,1)} %get-tuple-element.75), channel_id=1, source_target_pairs={{0,1},{1,0},{2,3},{3,2},{4,5},{5,4},{6,7},{7,6},{8,9},{9,8},{10,11... | collective-permute-start | bytes 7077896 | tf_op jit(solution)/shard_map/ppermute | solution.py:790
  190.9 12.0 %shard_map.213 = (bf16[4,96,3072]{2,1,0:T(8,128)(2,1)}, bf16[4,96,3072]{2,1,0:T(8,128)(2,1)}) custom-call(s32[1]{0:T(128)} %bitcast.17.own_ref, bf16[1344,768]{1,0:T(8,128)(2,1)} %get-tuple-element.68.refs_0_, bf16[1344,3072]{1,0:T(8,128)(2,1)} %get-tuple-element.69.refs_1_), custom_call_target="tpu_custom_call" | custom-call | flops 6341787648 | bytes 15040512 | tf_op jit(solution)/shard_map/pallas_call | solution.py:728
  202.9 1.4 copy-done.3
  204.3 3.3 add_convert_fusion
  207.7 30.2 %collective-permute-start.13 = (bf16[2,96,3072]{2,1,0:T(8,128)(2,1)S(1)}, bf16[2,96,3072]{2,1,0:T(8,128)(2,1)}, u32[]{:S(2)}, u32[]{:S(2)}) collective-permute-start(bf16[2,96,3072]{2,1,0:T(8,128)(2,1)S(1)} %slice.126), channel_id=1, source_target_pairs={{0,2},{1,3},{2,0},{3,1},{4,6},{5,7},{6,4},{7,5},{8,10},{9,11},{10,... | collective-permute-start | bytes 3538952 | tf_op jit(solution)/shard_map/ppermute | solution.py:790
  237.9 15.8 %shard_map.210.d_ref.refs_3_ = bf16[1344,2304]{1,0:T(8,128)(2,1)} custom-call(s32[4]{0:T(128)} %cls_ref.17, bf16[1344,2304]{1,0:T(8,128)(2,1)} %get-tuple-element.46.qkv_ref, bf16[1344,768]{1,0:T(8,128)(2,1)} %shard_map.204.o_ref.refs_0_, bf16[1344,768]{1,0:T(8,128)(2,1)} %get-tuple-element.55.do_ref), custom_call_target="tpu_custom_call" | custom-call | flops 16647192576 | bytes 16515072 | tf_op jit(solution)/shard_map/pallas_call | solution.py:615
  253.6 13.6 %shard_map.212 = (bf16[4,96,3072]{2,1,0:T(8,128)(2,1)}, bf16[4,96,3072]{2,1,0:T(8,128)(2,1)}) custom-call(s32[1]{0:T(128)} %bitcast.17.own_ref, bf16[1344,768]{1,0:T(8,128)(2,1)} %shard_map.204.o_ref.refs_0_, bf16[1344,768]{1,0:T(8,128)(2,1)} %get-tuple-element.64.refs_1_, bf16[1344,768]{1,0:T(8,128)(2,1)} %get-tuple-element.65.refs_2_, ...), custom_call_target="tpu_custom_call" | custom-call | flops 6341787648 | bytes 17104896 | tf_op jit(solution)/shard_map/pallas_call | solution.py:728
  267.3 5.8 %collective-permute-start.3 = (bf16[4,96,3072]{2,1,0:T(8,128)(2,1)}, bf16[4,96,3072]{2,1,0:T(8,128)(2,1)}, u32[]{:S(2)}, u32[]{:S(2)}) collective-permute-start(bf16[4,96,3072]{2,1,0:T(8,128)(2,1)} %get-tuple-element.67), channel_id=1, source_target_pairs={{0,1},{1,0},{2,3},{3,2},{4,5},{5,4},{6,7},{7,6},{8,9},{9,8},{10,11... | collective-permute-start | bytes 7077896 | tf_op jit(solution)/shard_map/ppermute | solution.py:790
  273.1 1.7 add_convert_fusion.4
  275.7 11.6 %shard_map.211 = (f32[1296,768]{1,0:T(8,128)}, f32[1,768]{1,0:T(1,128)}, f32[1,768]{1,0:T(1,128)}) custom-call(s32[4]{0:T(128)} %cls_ref.17, bf16[1344,2304]{1,0:T(8,128)(2,1)} %shard_map.210.d_ref.refs_3_, bf16[1344,768]{1,0:T(8,128)(2,1)} %get-tuple-element.45.x_ref, f32[1344,768]{1,0:T(8,128)} %get-tuple-element.56.gmid_ref, ...), custom_call_target="tpu_custom_call" | custom-call | flops 4756340736 | bytes 20054016 | tf_op jit(solution)/shard_map/pallas_call | solution.py:665
  287.3 1.3 concatenate.3
  288.7 1.7 copy.27
  290.4 6.7 %shard_map.208 = bf16[1296,768]{1,0:T(8,128)(2,1)} custom-call(s32[4]{0:T(128)} %cls_ref.17, f32[1344,768]{1,0:T(8,128)} %get-tuple-element.47.layer_ref, bf16[1344,768]{1,0:T(8,128)(2,1)} %get-tuple-element.50.o_ref.refs_0_, bf16[768,768]{1,0:T(8,128)(2,1)} %bitcast.43), custom_call_target="tpu_custom_call" | custom-call | flops 1585446912 | bytes 9437184 | tf_op jit(solution)/shard_map/pallas_call | solution.py:487
  297.1 66.1 %reduce-scatter.4.cloned.1.call-done = f32[96,6]{1,0:T(8,128)} async-done(((f32[768,6]{1,0:T(8,128)}), f32[96,6]{1,0:T(8,128)}) %reduce-scatter.4.cloned.1.call-update) | async-done | bytes 2320
  363.1 1.6 fusion
  367.6 1.3 add_bitcast_fusion
  369.2 2.2 add_convert_fusion.1
  371.6 1.4 collective-permute-start.10
  373.1 2.6 add_convert_fusion.3
  375.8 1.7 collective-permute-start.4
  377.5 0.9 add_convert_fusion.2
  378.5 1.6 collective-permute-start.7
  380.9 19.0 %collective-permute-done.10 = bf16[2,384,768]{2,1,0:T(8,128)(2,1)S(1)} collective-permute-done((bf16[2,384,768]{2,1,0:T(8,128)(2,1)S(1)}, bf16[2,384,768]{2,1,0:T(8,128)(2,1)S(1)}, u32[]{:S(2)}, u32[]{:S(2)}) %collective-permute-start.10) | collective-permute-done | bytes 1179680 | tf_op jit(solution)/shard_map/ppermute | solution.py:790
  400.2 1.6 collective-permute-start.11
  401.8 36.0 %collective-permute-done.4 = bf16[2,96,3072]{2,1,0:T(8,128)(2,1)S(1)} collective-permute-done((bf16[2,96,3072]{2,1,0:T(8,128)(2,1)S(1)}, bf16[2,96,3072]{2,1,0:T(8,128)(2,1)S(1)}, u32[]{:S(2)}, u32[]{:S(2)}) %collective-permute-start.4) | collective-permute-done | bytes 1179680 | tf_op jit(solution)/shard_map/ppermute | solution.py:790
  438.9 33.4 %collective-permute-done.7 = bf16[2,96,3072]{2,1,0:T(8,128)(2,1)S(1)} collective-permute-done((bf16[2,96,3072]{2,1,0:T(8,128)(2,1)S(1)}, bf16[2,96,3072]{2,1,0:T(8,128)(2,1)S(1)}, u32[]{:S(2)}, u32[]{:S(2)}) %collective-permute-start.7) | collective-permute-done | bytes 1179680 | tf_op jit(solution)/shard_map/ppermute | solution.py:790
  473.1 20.0 %collective-permute-done.5 = bf16[1,96,3072]{2,1,0:T(8,128)(2,1)S(1)} collective-permute-done((bf16[1,96,3072]{2,1,0:T(8,128)(2,1)S(1)}, bf16[1,96,3072]{2,1,0:T(8,128)(2,1)S(1)}, u32[]{:S(2)}, u32[]{:S(2)}) %collective-permute-start.5) | collective-permute-done | bytes 589856 | tf_op jit(solution)/shard_map/ppermute | solution.py:790
  494.0 1.1 convert_add_fusion
  495.1 1.0 slice_bitcast_fusion
  496.1 9.7 %collective-permute-done.8 = bf16[1,96,3072]{2,1,0:T(8,128)(2,1)S(1)} collective-permute-done((bf16[1,96,3072]{2,1,0:T(8,128)(2,1)S(1)}, bf16[1,96,3072]{2,1,0:T(8,128)(2,1)S(1)}, u32[]{:S(2)}, u32[]{:S(2)}) %collective-permute-start.8) | collective-permute-done | bytes 589856 | tf_op jit(solution)/shard_map/ppermute | solution.py:790
  505.7 1.2 convert_add_fusion.1
  (57 shorter events, 10.9 us)
Async XLA Ops:
  7.2 355.9 %reduce-scatter.4.cloned.1.call-start = ((), (), s32[]{:S(2)}) async-start(), calls=%async_computation.1 | async-start | bytes 442368
  7.2 78.4 %collective-permute-start.1 = (bf16[768,1536]{1,0:T(8,128)(2,1)}, bf16[768,1536]{1,0:T(8,128)(2,1)S(1)}, u32[]{:S(2)}, u32[]{:S(2)}) collective-permute-start(bf16[768,1536]{1,0:T(8,128)(2,1)} %bitcast.57), channel_id=1, source_target_pairs={{0,24},{8,0},{16,8},{24,16},{1,25},{9,1},{17,9},{25,17},{2,26},{10... | collective-permute-start | bytes 7077896 | tf_op jit(solution)/shard_map/ppermute | solution.py:806
  61.4 24.3 %collective-permute-start = (bf16[1344,768]{1,0:T(8,128)(2,1)}, bf16[1344,768]{1,0:T(8,128)(2,1)S(1)}, u32[]{:S(2)}, u32[]{:S(2)}) collective-permute-start(bf16[1344,768]{1,0:T(8,128)(2,1)} %get-tuple-element.48.refs_1_), channel_id=1, source_target_pairs={{0,24},{8,0},{16,8},{24,16},{1,25},{9,1},{17,9},{25,17},{2,26},{10... | collective-permute-start | bytes 6193160 | tf_op jit(solution)/shard_map/ppermute | solution.py:806
  85.6 1.3 copy-start.10
  85.6 2.1 copy-start.8
  113.2 25.4 %collective-permute-start.2 = (bf16[1344,768]{1,0:T(8,128)(2,1)}, bf16[1344,768]{1,0:T(8,128)(2,1)S(1)}, u32[]{:S(2)}, u32[]{:S(2)}) collective-permute-start(bf16[1344,768]{1,0:T(8,128)(2,1)} %get-tuple-element.52), channel_id=1, source_target_pairs={{0,8},{8,16},{16,24},{24,0},{1,9},{9,17},{17,25},{25,1},{2,10},{10... | collective-permute-start | bytes 6193160 | tf_op jit(solution)/shard_map/ppermute | solution.py:806
  127.8 75.1 %collective-permute-start.12 = (bf16[4,96,3072]{2,1,0:T(8,128)(2,1)}, bf16[4,96,3072]{2,1,0:T(8,128)(2,1)S(1)}, u32[]{:S(2)}, u32[]{:S(2)}) collective-permute-start(bf16[4,96,3072]{2,1,0:T(8,128)(2,1)} %get-tuple-element.78), channel_id=1, source_target_pairs={{0,1},{1,0},{2,3},{3,2},{4,5},{5,4},{6,7},{7,6},{8,9},{9,8},{10,11... | collective-permute-start | bytes 7077896 | tf_op jit(solution)/shard_map/ppermute | solution.py:790
  138.6 1.3 copy-start.9
  183.5 185.8 %collective-permute-start.9 = (bf16[4,384,768]{2,1,0:T(8,128)(2,1)}, bf16[4,384,768]{2,1,0:T(8,128)(2,1)}, u32[]{:S(2)}, u32[]{:S(2)}) collective-permute-start(bf16[4,384,768]{2,1,0:T(8,128)(2,1)} %get-tuple-element.75), channel_id=1, source_target_pairs={{0,1},{1,0},{2,3},{3,2},{4,5},{5,4},{6,7},{7,6},{8,9},{9,8},{10,11... | collective-permute-start | bytes 7077896 | tf_op jit(solution)/shard_map/ppermute | solution.py:790
  202.9 174.6 %collective-permute-start.6 = (bf16[4,96,3072]{2,1,0:T(8,128)(2,1)}, bf16[4,96,3072]{2,1,0:T(8,128)(2,1)S(1)}, u32[]{:S(2)}, u32[]{:S(2)}) collective-permute-start(bf16[4,96,3072]{2,1,0:T(8,128)(2,1)} %get-tuple-element.71), channel_id=1, source_target_pairs={{0,1},{1,0},{2,3},{3,2},{4,5},{5,4},{6,7},{7,6},{8,9},{9,8},{10,11... | collective-permute-start | bytes 7077896 | tf_op jit(solution)/shard_map/ppermute | solution.py:790
  202.9 1.4 copy-start.3
  207.7 65.4 %collective-permute-start.13 = (bf16[2,96,3072]{2,1,0:T(8,128)(2,1)S(1)}, bf16[2,96,3072]{2,1,0:T(8,128)(2,1)}, u32[]{:S(2)}, u32[]{:S(2)}) collective-permute-start(bf16[2,96,3072]{2,1,0:T(8,128)(2,1)S(1)} %slice.126), channel_id=1, source_target_pairs={{0,2},{1,3},{2,0},{3,1},{4,6},{5,7},{6,4},{7,5},{8,10},{9,11},{10,... | collective-permute-start | bytes 3538952 | tf_op jit(solution)/shard_map/ppermute | solution.py:790
  267.3 105.7 %collective-permute-start.3 = (bf16[4,96,3072]{2,1,0:T(8,128)(2,1)}, bf16[4,96,3072]{2,1,0:T(8,128)(2,1)}, u32[]{:S(2)}, u32[]{:S(2)}) collective-permute-start(bf16[4,96,3072]{2,1,0:T(8,128)(2,1)} %get-tuple-element.67), channel_id=1, source_target_pairs={{0,1},{1,0},{2,3},{3,2},{4,5},{5,4},{6,7},{7,6},{8,9},{9,8},{10,11... | collective-permute-start | bytes 7077896 | tf_op jit(solution)/shard_map/ppermute | solution.py:790
  275.7 91.9 %collective-permute-start.14 = (bf16[1,96,3072]{2,1,0:T(8,128)(2,1)}, bf16[1,96,3072]{2,1,0:T(8,128)(2,1)}, u32[]{:S(2)}, u32[]{:S(2)}) collective-permute-start(bf16[1,96,3072]{2,1,0:T(8,128)(2,1)} %slice.128), channel_id=1, source_target_pairs={{0,4},{1,5},{2,6},{3,7},{4,0},{5,1},{6,2},{7,3},{8,12},{9,13},{10,... | collective-permute-start | bytes 1769480 | tf_op jit(solution)/shard_map/ppermute | solution.py:790
  275.7 11.6 %copy-start.4 = (f32[1,768]{1,0:T(1,128)S(1)}, f32[1,768]{1,0:T(1,128)}, u32[]{:S(2)}) copy-start(f32[1,768]{1,0:T(1,128)} %get-tuple-element.60) | copy-start | bytes 9220
  275.7 11.6 %copy-start.5 = (f32[1,768]{1,0:T(1,128)S(1)}, f32[1,768]{1,0:T(1,128)}, u32[]{:S(2)}) copy-start(f32[1,768]{1,0:T(1,128)} %get-tuple-element.63) | copy-start | bytes 9220
  275.7 11.6 %copy-start.6 = (f32[1,768]{1,0:T(1,128)S(1)}, f32[1,768]{1,0:T(1,128)}, u32[]{:S(2)}) copy-start(f32[1,768]{1,0:T(1,128)} %get-tuple-element.59) | copy-start | bytes 9220
  275.7 11.6 %copy-start.7 = (f32[1,768]{1,0:T(1,128)S(1)}, f32[1,768]{1,0:T(1,128)}, u32[]{:S(2)}) copy-start(f32[1,768]{1,0:T(1,128)} %get-tuple-element.62) | copy-start | bytes 9220
  367.0 2.2 copy-start.1
  369.0 11.9 %collective-permute-start.15 = (f32[96,1536]{1,0:T(8,128)S(1)}, f32[96,1536]{1,0:T(8,128)S(1)}, u32[]{:S(2)}, u32[]{:S(2)}) collective-permute-start(f32[96,1536]{1,0:T(8,128)S(1)} %slice.130), channel_id=1, source_target_pairs={{0,8},{8,16},{16,24},{24,0},{1,9},{9,17},{17,25},{25,1},{2,10},{10... | collective-permute-start | bytes 1769480 | tf_op jit(solution)/shard_map/ppermute | solution.py:806
  371.5 1.7 copy-start.2
  371.6 28.3 %collective-permute-start.10 = (bf16[2,384,768]{2,1,0:T(8,128)(2,1)S(1)}, bf16[2,384,768]{2,1,0:T(8,128)(2,1)S(1)}, u32[]{:S(2)}, u32[]{:S(2)}) collective-permute-start(bf16[2,384,768]{2,1,0:T(8,128)(2,1)S(1)} %slice.122), channel_id=1, source_target_pairs={{0,2},{1,3},{2,0},{3,1},{4,6},{5,7},{6,4},{7,5},{8,10},{9,11},{10,... | collective-permute-start | bytes 3538952 | tf_op jit(solution)/shard_map/ppermute | solution.py:790
  375.7 1.8 copy-start
  375.8 62.0 %collective-permute-start.4 = (bf16[2,96,3072]{2,1,0:T(8,128)(2,1)S(1)}, bf16[2,96,3072]{2,1,0:T(8,128)(2,1)S(1)}, u32[]{:S(2)}, u32[]{:S(2)}) collective-permute-start(bf16[2,96,3072]{2,1,0:T(8,128)(2,1)S(1)} %slice.112), channel_id=1, source_target_pairs={{0,2},{1,3},{2,0},{3,1},{4,6},{5,7},{6,4},{7,5},{8,10},{9,11},{10,... | collective-permute-start | bytes 3538952 | tf_op jit(solution)/shard_map/ppermute | solution.py:790
  378.5 93.8 %collective-permute-start.7 = (bf16[2,96,3072]{2,1,0:T(8,128)(2,1)S(1)}, bf16[2,96,3072]{2,1,0:T(8,128)(2,1)S(1)}, u32[]{:S(2)}, u32[]{:S(2)}) collective-permute-start(bf16[2,96,3072]{2,1,0:T(8,128)(2,1)S(1)} %slice.118), channel_id=1, source_target_pairs={{0,2},{1,3},{2,0},{3,1},{4,6},{5,7},{6,4},{7,5},{8,10},{9,11},{10,... | collective-permute-start | bytes 3538952 | tf_op jit(solution)/shard_map/ppermute | solution.py:790
  400.2 93.7 %collective-permute-start.11 = (bf16[1,384,768]{2,1,0:T(8,128)(2,1)S(1)}, bf16[1,384,768]{2,1,0:T(8,128)(2,1)S(1)}, u32[]{:S(2)}, u32[]{:S(2)}) collective-permute-start(bf16[1,384,768]{2,1,0:T(8,128)(2,1)S(1)} %slice.124), channel_id=1, source_target_pairs={{0,4},{1,5},{2,6},{3,7},{4,0},{5,1},{6,2},{7,3},{8,12},{9,13},{10,... | collective-permute-start | bytes 1769480 | tf_op jit(solution)/shard_map/ppermute | solution.py:790
  438.3 54.8 %collective-permute-start.5 = (bf16[1,96,3072]{2,1,0:T(8,128)(2,1)S(1)}, bf16[1,96,3072]{2,1,0:T(8,128)(2,1)S(1)}, u32[]{:S(2)}, u32[]{:S(2)}) collective-permute-start(bf16[1,96,3072]{2,1,0:T(8,128)(2,1)S(1)} %slice.114), channel_id=1, source_target_pairs={{0,4},{1,5},{2,6},{3,7},{4,0},{5,1},{6,2},{7,3},{8,12},{9,13},{10,... | collective-permute-start | bytes 1769480 | tf_op jit(solution)/shard_map/ppermute | solution.py:790
  472.8 33.0 %collective-permute-start.8 = (bf16[1,96,3072]{2,1,0:T(8,128)(2,1)S(1)}, bf16[1,96,3072]{2,1,0:T(8,128)(2,1)S(1)}, u32[]{:S(2)}, u32[]{:S(2)}) collective-permute-start(bf16[1,96,3072]{2,1,0:T(8,128)(2,1)S(1)} %slice.120), channel_id=1, source_target_pairs={{0,4},{1,5},{2,6},{3,7},{4,0},{5,1},{6,2},{7,3},{8,12},{9,13},{10,... | collective-permute-start | bytes 1769480 | tf_op jit(solution)/shard_map/ppermute | solution.py:790
Sparse Core Ops, SparseCore 0:
  290.5 72.6 reduce-scatter.3

commit v2 on v1

v2 whole, which is shorter than its diff:
```python
import functools

import jax
import jax.numpy as jnp
from jax import lax
from jax.experimental import pallas as pl
from jax.experimental.pallas import tpu as pltpu
from jax.sharding import PartitionSpec as P

HEADS = 12
HEAD = 64
SLOT = 324
CLASSES = ((112, 100), (208, 196), (336, 324))
MOST = 336
EPS = 1e-05
GELU_A = 0.7978845608028654
GELU_B = 0.044715
BF = jnp.bfloat16
F32 = jnp.float32


def dot(left, right, left_dim, right_dim):
    return lax.dot_general(
        left, right, (((left_dim,), (right_dim,)), ((), ())), preferred_element_type=F32
    )


def params(limit_mib=20):
    return pltpu.CompilerParams(vmem_limit_bytes=limit_mib * 2**20)


def cost(flops, moved):
    return pl.CostEstimate(flops=int(flops) // 2000, bytes_accessed=int(moved) // 2000, transcendentals=0)


def rows_of(item):
    return 112 + jnp.where(item >= 1, 96, 0) + jnp.where(item >= 2, 128, 0)


def start_of(cls_ref, clip):
    start = jnp.int32(0)
    for before in range(clip):
        start = start + rows_of(cls_ref[before])
    return pl.multiple_of(start, 16)


def start_dyn(cls_ref, clip, clips):
    start = jnp.int32(0)
    for before in range(clips):
        start = start + jnp.where(before < clip, rows_of(cls_ref[before]), 0)
    return pl.multiple_of(start, 16)


def total_of(cls_ref, clips):
    return start_of(cls_ref, clips)


def clear_from(total, refs):
    rows = refs[0].shape[0]

    @pl.loop(0, (rows - total) // 16)
    def _(step):
        at = pl.ds(pl.multiple_of(total + step * 16, 16), 16)
        for ref in refs:
            ref[at, :] = jnp.zeros((16, ref.shape[1]), ref.dtype)


def clear_tail(cls_ref, clips, refs):
    clear_from(total_of(cls_ref, clips), refs)


def merge(first, second, base, target):
    half = first.shape[0]
    target[:half, :] = first[...]
    target[half:, :] = jnp.zeros((target.shape[0] - half, target.shape[1]), target.dtype)
    target[pl.ds(base, half), :] = second[...]


def by_class(item, body):
    for index, (rows, live) in enumerate(CLASSES):
        pl.when(item == index)(functools.partial(body, rows, live))


def norm_stats(values):
    centre = jnp.mean(values, -1, keepdims=True)
    centred = values - centre
    spread = jnp.mean(centred * centred, -1, keepdims=True)
    root = lax.rsqrt(spread + EPS)
    return centred * root, root


def norm_back(values, gain, grad, gain_acc, bias_acc):
    unit, root = norm_stats(values)
    gain_acc[...] += jnp.sum(grad * unit, 0, keepdims=True)
    bias_acc[...] += jnp.sum(grad, 0, keepdims=True)
    scaled = grad * gain
    return root * (
        scaled
        - jnp.mean(scaled, -1, keepdims=True)
        - unit * jnp.mean(scaled * unit, -1, keepdims=True)
    )


def interleave(stages, count):
    held = [dict() for _ in range(count)]
    for step in range(count + len(stages) - 1):
        for index, stage in enumerate(stages):
            if 0 <= step - index < count:
                stage(step - index, held[step - index])


def one_head(pair, head):
    lane = lax.broadcasted_iota(jnp.int32, pair.shape, 1)
    keep = lane < HEAD if head % 2 == 0 else lane >= HEAD
    return jnp.where(keep, pair, jnp.zeros_like(pair))


def pair_of(head):
    return slice(128 * (head // 2), 128 * (head // 2) + 128)


def mask_keys_lane(scores, live):
    lane = lax.broadcasted_iota(jnp.int32, scores.shape, 1)
    return jnp.where(lane < live, scores, -1e30)


def mask_keys_row(scores, live):
    head, tail = scores[:-16], scores[-16:]
    row = lax.broadcasted_iota(jnp.int32, tail.shape, 0)
    tail = jnp.where(row < live - head.shape[0], tail, -1e30)
    return jnp.concatenate([head, tail], axis=0)


def attend(load_q, load_k, load_v, store, live):
    pairs = {}

    def score(head, held):
        query = one_head(load_q(head), head) * jnp.asarray(HEAD**-0.5, BF)
        held["s"] = mask_keys_lane(dot(query, load_k(head), 1, 1), live)

    def soften(head, held):
        scores = held.pop("s")
        exps = jnp.exp(scores - jnp.max(scores, -1, keepdims=True))
        held["l"] = jnp.sum(exps, -1, keepdims=True)
        held["e"] = exps.astype(BF)

    def mix(head, held):
        mixed = dot(held.pop("e"), one_head(load_v(head), head), 1, 0) / held.pop("l")
        if head % 2 == 0:
            pairs[head // 2] = mixed
        else:
            store(head, (pairs.pop(head // 2) + mixed).astype(BF))

    interleave([score, soften, mix], HEADS)


def attend_back(load_q, load_k, load_v, load_do, load_o, store, live):
    cache = {}

    def turned(head, name, load, wide=False):
        key = (name, head // 2)
        if key not in cache:
            value = load(head).T
            cache[key] = value.astype(F32) if wide else value
        at = HEAD * (head % 2)
        return cache[key][at : at + HEAD]

    def score(head, held):
        held["q"] = one_head(load_q(head), head) * jnp.asarray(HEAD**-0.5, BF)
        held["s"] = mask_keys_row(dot(load_k(head), held["q"], 1, 1), live)
        held["do"] = one_head(load_do(head), head)
        held["dp"] = dot(load_v(head), held["do"], 1, 1)

    def soften(head, held):
        scores = held.pop("s")
        exps = jnp.exp(scores - jnp.max(scores, 0, keepdims=True))
        held["p"] = exps * (1.0 / jnp.sum(exps, 0, keepdims=True))
        held["pb"] = held["p"].astype(BF)

    def mix(head, held):
        if load_o is None:
            held["o"] = dot(turned(head, "v", load_v), held["pb"], 1, 0)
        else:
            held["o"] = turned(head, "o", load_o, True)

    def grad_score(head, held):
        row_terms = jnp.sum(held["o"] * turned(head, "do", load_do, True), 0, keepdims=True)
        held["ds"] = (held.pop("p") * (held.pop("dp") - row_terms)).astype(BF)

    def finish(head, held):
        grad = held.pop("ds")
        held["dv"] = dot(held.pop("pb"), held.pop("do"), 1, 0)
        held["dk"] = dot(grad, held.pop("q"), 1, 0)
        held["dq"] = dot(turned(head, "k", load_k), grad, 1, 0) * HEAD**-0.5
        if head % 2 == 0:
            cache["half"] = held
            return
        first = cache.pop("half")
        mixed = None
        if load_o is None:
            mixed = jnp.concatenate([first["o"], held["o"]], 0).astype(BF).T
        query = jnp.concatenate([first["dq"], held["dq"]], 0).astype(BF).T
        store(
            head,
            query,
            (first["dk"] + held["dk"]).astype(BF),
            (first["dv"] + held["dv"]).astype(BF),
            mixed,
        )

    interleave([score, soften, mix, grad_score, finish], HEADS)


def in_hbm(shape, kind):
    return pltpu.HBM(shape, kind)


def bits_of(count):
    return count.bit_length() - 1


def place_to_part(place, order):
    part = 0
    for index, bit in enumerate(order):
        if place >> (len(order) - 1 - index) & 1:
            part |= 1 << bit
    return part


def part_to_place(distance, order):
    place = jnp.int32(0)
    for position, bit in enumerate(order):
        place = place | (((distance >> bit) & 1) << (len(order) - 1 - position))
    return place


def product_block(acc, left, right):
    acc[...] = dot(left[...], right[...], 0, 0).astype(BF)


def put_part(part, distance, order, kept, sent):
    half = kept.shape[0]
    place = part_to_place(distance, order)

    @pl.when(place < half)
    def _():
        kept[jnp.minimum(place, half - 1)] = part

    @pl.when(place >= half)
    def _():
        sent[jnp.maximum(place - half, 0)] = part


def put_parts(acc, own, shards, order, kept, sent):
    part_rows = acc.shape[0] // shards
    half = shards // 2
    for place in range(shards):
        if part_rows % 16:
            part = acc[place * part_rows : (place + 1) * part_rows, :]
            put_part(part, own ^ place, order, kept, sent)
            continue
        owner = own ^ place_to_part(place, order)
        at = pl.ds(pl.multiple_of(owner * part_rows, 16), part_rows)
        if place < half:
            kept[place] = acc[at, :]
        else:
            sent[place - half] = acc[at, :]


def put_parts_tall(acc, own, orders, bounds, outs, block):
    part_rows = outs[0].shape[1]
    per_block = acc.shape[0] // part_rows
    for sub in range(per_block):
        distance = own ^ (block * per_block + sub)
        for kind, order in enumerate(orders):
            kept, sent = outs[2 * kind : 2 * kind + 2]
            part = acc[sub * part_rows : (sub + 1) * part_rows, bounds[kind] : bounds[kind + 1]]
            put_part(part, distance, order, kept, sent)


def part_outs(shards, part_rows, width, bounds, lead):
    half = shards // 2
    specs, shapes = [], []
    for low, high in zip(bounds, bounds[1:]):
        for _ in range(2):

            def index(j, *_, low=low, high=high):
                return (0, 0, jnp.clip(j - lead, low, high - 1) - low)

            specs.append(pl.BlockSpec((half, part_rows, width), index))
            shapes.append(in_hbm((half, part_rows, width * (high - low)), BF))
    return specs, shapes


def pack_clip(cls_ref, clip, source, target, masked):
    start = start_of(cls_ref, clip)

    def copy(rows, live):
        held = min(rows, SLOT)
        value = source[clip * SLOT : clip * SLOT + held, :]
        if masked:
            row = lax.broadcasted_iota(jnp.int32, value.shape, 0)
            value = jnp.where(row < live, value, jnp.zeros_like(value))
        if rows > held:
            pad = jnp.zeros((rows - held, value.shape[1]), value.dtype)
            value = jnp.concatenate([value, pad], 0)
        target[pl.ds(start, rows), :] = value

    by_class(cls_ref[clip], copy)


def call(kernel, scalars, grid, in_specs, operands, after=(), scratch=(), limit=20, **options):
    scalars, operands, after = list(scalars), list(operands), jax.tree.leaves(after)
    known = len(scalars) + len(operands)

    def body(*refs):
        kernel(*refs[:known], *refs[known + len(after) :])

    return pl.pallas_call(
        body,
        grid_spec=pltpu.PrefetchScalarGridSpec(
            num_scalar_prefetch=len(scalars),
            grid=grid,
            in_specs=list(in_specs) + [pl.BlockSpec(memory_space=pl.ANY)] * len(after),
            out_specs=options.pop("out_specs"),
            scratch_shapes=list(scratch),
        ),
        compiler_params=params(limit),
        **options,
    )(*scalars, *operands, *after)


def whole(shape):
    del shape
    return pl.BlockSpec(memory_space=pltpu.VMEM)


def whole_out(shape):
    del shape
    return pl.BlockSpec(memory_space=pltpu.VMEM)


def tile(rows, columns):
    return pl.BlockSpec((rows, columns), lambda i, *_: (i, 0))


def in_main(value):
    return pltpu.with_memory_space_constraint(value, pltpu.HBM)


def pack_grad(cotangent, classes, rows, w_out, after=()):
    clips = classes.shape[0]
    width = cotangent.shape[1]

    def kernel(cls_ref, source, out_w, target, do_ref):
        for clip in range(clips):
            pack_clip(cls_ref, clip, source, target, True)
        clear_tail(cls_ref, clips, [target, do_ref])
        for clip in range(clips):
            start = start_of(cls_ref, clip)

            def body(count, live):
                at = pl.ds(start, count)
                do_ref[at, :] = dot(target[at, :], out_w[...], 1, 1).astype(BF)

            by_class(cls_ref[clip], body)

    return call(
        kernel,
        [classes],
        (1,),
        [whole(cotangent.shape), whole(w_out.shape)],
        [cotangent, w_out],
        after,
        limit=20,
        out_specs=[whole_out((rows, width))] * 2,
        out_shape=[jax.ShapeDtypeStruct((rows, width), BF)] * 2,
        cost_estimate=cost(2 * rows * width * width, 6 * rows * width),
    )


def norm_project(tokens, classes, rows, gain, bias, weight, step, after=()):
    clips = classes.shape[0]
    width, wide = weight.shape

    def kernel(cls_ref, tok_ref, gain_ref, bias_ref, w_ref, x_ref, h_ref, qkv_ref):
        index = pl.program_id(0)

        @pl.when(index == 0)
        def _():
            for clip in range(clips):
                pack_clip(cls_ref, clip, tok_ref, x_ref, False)
            clear_tail(cls_ref, clips, [x_ref])

        live = index * step < total_of(cls_ref, clips)

        @pl.when(live)
        def _():
            at = pl.ds(pl.multiple_of(index * step, 16), step)
            unit, _ = norm_stats(x_ref[at, :].astype(F32))
            low = (unit * gain_ref[:, :width] + bias_ref[:, :width]).astype(BF)
            h_ref[...] = low
            qkv_ref[...] = dot(low, w_ref[...], 1, 0).astype(BF)

        @pl.when(jnp.logical_not(live))
        def _():
            h_ref[...] = jnp.zeros_like(h_ref)
            qkv_ref[...] = jnp.zeros_like(qkv_ref)

    return call(
        kernel,
        [classes],
        (rows // step,),
        [whole(tokens.shape), whole(gain.shape), whole(bias.shape), whole(weight.shape)],
        [tokens, gain, bias, weight],
        after,
        limit=20,
        out_specs=[whole_out((rows, width)), tile(step, width), tile(step, wide)],
        out_shape=[
            jax.ShapeDtypeStruct((rows, width), BF),
            in_hbm((rows, width), BF),
            jax.ShapeDtypeStruct((rows, wide), BF),
        ],
        cost_estimate=cost(2 * rows * width * wide, 2 * rows * (3 * width + wide) + 2 * weight.size),
    )


def self_attend(qkv, classes, after=()):
    clips = classes.shape[0]
    rows, wide = qkv.shape
    width = wide // 3

    def kernel(cls_ref, qkv_ref, o_ref):
        clip = pl.program_id(0)
        start = start_dyn(cls_ref, clip, clips)

        def body(count, live):
            at = pl.ds(start, count)

            def load(part):
                def get(head):
                    pair = pair_of(head)
                    return qkv_ref[at, part * width + pair.start : part * width + pair.stop]

                return get

            def store(head, mixed):
                o_ref[at, pair_of(head)] = mixed

            attend(load(0), load(1), load(2), store, live)

        by_class(cls_ref[clip], body)

        @pl.when(clip == clips - 1)
        def _():
            clear_tail(cls_ref, clips, [o_ref])

    return call(
        kernel,
        [classes],
        (clips,),
        [whole(qkv.shape)],
        [qkv],
        after,
        limit=20,
        out_specs=whole_out((rows, width)),
        out_shape=jax.ShapeDtypeStruct((rows, width), BF),
        cost_estimate=cost(16 * rows * MOST * width, 2 * rows * (wide + width)),
    )


def feed_forward(x, mixed, classes, gains, biases, w_out, w_up, w_down, w_fq, step, tiles, done=None, after=()):
    clips = classes.shape[0]
    rows, width = x.shape
    hidden = w_up.shape[1]
    chunk = width
    first, last = tiles
    shapes = [(width, F32), (width, BF), (hidden, BF), (hidden, BF), (width, F32), (width, BF), (width, BF)]
    count = 0 if done is None else len(shapes)

    def kernel(cls_ref, x_ref, o_ref, gain_ref, bias_ref, out_w, up_w, down_w, fq_w, *refs):
        mid_ref, h_ref, u_ref, act_ref, layer_ref, n_ref, fq_ref, part_ref = refs[count:]
        live = (first + pl.program_id(0)) * step < total_of(cls_ref, clips)

        @pl.when(live)
        def _():
            middle = x_ref[...].astype(F32) + dot(o_ref[...], out_w[...], 1, 0)
            mid_ref[...] = middle
            unit, _ = norm_stats(middle)
            low = (unit * gain_ref[:, width : 2 * width] + bias_ref[:, width : 2 * width]).astype(BF)
            h_ref[...] = low
            layer = middle
            for at in range(0, hidden, chunk):
                part = slice(at, at + chunk)
                up = dot(low, up_w[:, part], 1, 0)
                inner = jnp.tanh(GELU_A * (up + GELU_B * (up * up * up)))
                act = (0.5 * up * (1.0 + inner)).astype(BF)
                u_ref[:, part] = up.astype(BF)
                act_ref[:, part] = act
                layer = layer + dot(act, down_w[part, :], 1, 0)
            layer_ref[...] = layer
            unit, _ = norm_stats(layer)
            low = (unit * gain_ref[:, 2 * width :] + bias_ref[:, 2 * width :]).astype(BF)
            n_ref[...] = low
            part_ref[...] = low
            fq_ref[...] = dot(low, fq_w[...], 1, 0).astype(BF)

        @pl.when(jnp.logical_not(live))
        def _():
            for ref in (mid_ref, h_ref, u_ref, act_ref, layer_ref, n_ref, fq_ref, part_ref):
                ref[...] = jnp.zeros_like(ref)

    weights = [w_out, w_up, w_down, w_fq]
    operands = [classes, x, mixed, gains, biases, *weights] + list(done or [])
    share = (last - first) * step

    def part_tile(columns):
        return pl.BlockSpec((step, columns), lambda i, *_: (first + i, 0))

    return call(
        kernel,
        operands[:1],
        (last - first,),
        [part_tile(width), part_tile(width), whole(gains.shape), whole(biases.shape)]
            + [whole(w.shape) for w in weights]
            + [pl.BlockSpec(memory_space=pl.ANY)] * count,
        operands[1:],
        after,
        limit=20,
        out_specs=[part_tile(columns) for columns, _ in shapes] + [tile(step, width)],
        out_shape=[in_hbm((rows, columns), kind) for columns, kind in shapes] + [in_hbm((share, width), BF)],
        input_output_aliases={len(operands) - count + i: i for i in range(count)},
        cost_estimate=cost(
            2 * share * sum(w.size for w in weights),
            2 * sum(w.size for w in weights) + share * (4 * 5 * width + 4 * hidden),
        ),
    )


def join_attend(arrived, fq, grad_mixed, w_kv, classes, first, last, after=()):
    clips = classes.shape[0]
    rows, width = fq.shape
    wide = w_kv.shape[1]
    parts = len(arrived)
    share = (last - first) * MOST

    def kernel(cls_ref, *refs):
        pieces = refs[:parts]
        q_ref, do_ref, kv_w, o_ref, dq_ref, dn_ref, dkv_ref = refs[parts : parts + 7]
        kv = refs[-1]
        n_ref = refs[parts + 7] if parts > 1 else pieces[0]
        clip = first + pl.program_id(0)
        start = start_dyn(cls_ref, clip, clips)
        base = start_of(cls_ref, first)

        if parts > 1:

            @pl.when(clip == first)
            def _():
                at = 0
                for piece in pieces:
                    n_ref[at : at + piece.shape[0], :] = piece[...]
                    at += piece.shape[0]

        def body(count, live):
            at = pl.ds(start, count)
            to = pl.ds(pl.multiple_of(start - base, 16), count)
            kv[:count, :] = dot(n_ref[at, :], kv_w[...], 1, 0).astype(BF)

            def load_k(head):
                return kv[:count, pair_of(head)]

            def load_v(head):
                pair = pair_of(head)
                return kv[:count, width + pair.start : width + pair.stop]

            def store(head, query, key, value, mixed):
                pair = pair_of(head)
                o_ref[to, pair] = mixed
                dq_ref[to, pair] = query
                dkv_ref[to, pair] = key
                dkv_ref[to, width + pair.start : width + pair.stop] = value

            attend_back(
                lambda head: q_ref[at, pair_of(head)],
                load_k,
                load_v,
                lambda head: do_ref[at, pair_of(head)],
                None,
                store,
                live,
            )
            dn_ref[to, :] = dot(dkv_ref[to, :], kv_w[...], 1, 1).astype(BF)

        by_class(cls_ref[clip], body)

        @pl.when(clip == last - 1)
        def _():
            clear_from(start_of(cls_ref, last) - base, [o_ref, dq_ref, dkv_ref, dn_ref])

    operands = [*arrived, fq, grad_mixed, w_kv]
    return call(
        kernel,
        [classes],
        (last - first,),
        [whole(v.shape) for v in operands],
        [*operands],
        after,
        limit=24,
        out_specs=[whole_out((share, width))] * (4 if parts == 1 else 5),
        scratch=[pltpu.VMEM((MOST, wide), BF)],
        out_shape=[
            in_hbm((share, width), BF), in_hbm((share, width), BF), jax.ShapeDtypeStruct((share, width), BF),
            in_hbm((share, wide), BF),
        ]
        + ([jax.ShapeDtypeStruct((rows, width), BF)] if parts > 1 else []),
        cost_estimate=cost(32 * rows * MOST * width, 10 * rows * width),
    )


def join_weights(own, products, classes, shards, order, after=()):
    clips = classes.shape[0]
    flat, places = [], []

    def place(value):
        for at, held in enumerate(flat):
            if held is value:
                return at
        flat.append(value)
        return len(flat) - 1

    for left, right, column in products:
        places.append(([place(v) for v in left], [place(v) for v in right], column))
    width = products[0][0][0].shape[1]
    share = min(v.shape[0] for v in flat)
    specs, shapes = part_outs(shards, width // shards, width, [0, len(products)], 0)

    def kernel(cls_ref, own_ref, *refs):
        kept, sent, acc = refs[-3:]
        index = pl.program_id(0)
        tail = pl.ds(start_of(cls_ref, clips // 2), share)

        def pieces(at, column):
            part = slice(column * width, (column + 1) * width)
            if len(at) == 2:
                return refs[at[0]][:, part], refs[at[1]][:, part]
            return refs[at[0]][:share, part], refs[at[0]][tail, part]

        for block, (left, right, column) in enumerate(places):

            @pl.when(index == block)
            def _():
                left_head, left_tail = pieces(left, 0)
                right_head, right_tail = pieces(right, column)
                acc[...] = (dot(left_head, right_head, 0, 0) + dot(left_tail, right_tail, 0, 0)).astype(BF)

        put_parts(acc, own_ref[0], shards, order, kept, sent)

    out = call(
        kernel,
        [classes, own],
        (len(products),),
        [whole(v.shape) for v in flat],
        flat,
        after,
        limit=24,
        out_specs=specs,
        scratch=[pltpu.VMEM((width, width), BF)],
        out_shape=shapes,
        cost_estimate=cost(2 * share * width * width, 4 * share * width),
    )
    return Sum(*out, order)


def join_result(layer, mixed, w_out, classes, slots, after=()):
    clips = classes.shape[0]
    rows, width = layer.shape

    def kernel(cls_ref, layer_ref, oa, ob, w_ref, out_ref):
        for clip in range(clips):
            start = start_of(cls_ref, clip)
            o_ref = oa if clip < clips // 2 else ob
            base = 0 if clip < clips // 2 else start_of(cls_ref, clips // 2)

            def body(count, live, start=start, base=base, o_ref=o_ref, clip=clip):
                at = pl.ds(start, count)
                from_at = pl.ds(pl.multiple_of(start - base, 16), count)
                value = layer_ref[at, :] + dot(o_ref[from_at, :], w_ref[...], 1, 0)
                held = min(count, SLOT)
                row = lax.broadcasted_iota(jnp.int32, value.shape, 0)
                value = jnp.where(row < live, value, 0.0).astype(BF)
                first = clip * SLOT
                out_ref[first : first + held, :] = value[:held]
                if held < SLOT:
                    out_ref[first + held : first + SLOT, :] = jnp.zeros((SLOT - held, width), BF)

            by_class(cls_ref[clip], body)

    return call(
        kernel,
        [classes],
        (1,),
        [whole(v.shape) for v in (layer, *mixed, w_out)],
        [layer, *mixed, w_out],
        after,
        limit=20,
        out_specs=whole_out((slots, width)),
        out_shape=jax.ShapeDtypeStruct((slots, width), BF),
        cost_estimate=cost(2 * rows * width * width, 8 * rows * width + 2 * w_out.size),
    )


def join_back(own, dfq, back, layer, grad, act, classes, gains, w_fq, step, shards, orders, cuts, after=()):
    clips = classes.shape[0]
    rows, width = layer.shape
    tall = act.shape[1]
    blocks = tall // width
    tiles = rows // step
    bounds = [*cuts, width]
    half = shards // 2
    outs_shapes = [
        jax.ShapeDtypeStruct((half, tall // shards, bounds[k + 1] - bounds[k]), BF) for k in range(len(orders)) for _ in range(2)
    ]

    def kernel(
        cls_ref, own_ref, dfqa, dfqb, backa, backb, layer_ref, g_ref, act_ref, gain_ref, fq_w,
        out_ref, gain_acc, bias_acc, *refs,
    ):
        outs = refs[:-4]
        dfq_ref, back_ref, low_ref, acc = refs[-4:]
        index = pl.program_id(0)

        @pl.when(index == 0)
        def _():
            gain_acc[...] = jnp.zeros_like(gain_acc)
            bias_acc[...] = jnp.zeros_like(bias_acc)
            base = start_of(cls_ref, clips // 2)
            merge(dfqa, dfqb, base, dfq_ref)
            merge(backa, backb, base, back_ref)

        total = total_of(cls_ref, clips)
        live = index * step < total
        at = pl.ds(pl.multiple_of(jnp.minimum(index, tiles - 1) * step, 16), step)

        @pl.when((index < tiles) & live)
        def _():
            grad_norm = dot(dfq_ref[at, :], fq_w[...], 1, 1) + back_ref[at, :].astype(F32)
            grad_layer = g_ref[...].astype(F32) + norm_back(
                layer_ref[...], gain_ref[:, 2 * width :], grad_norm, gain_acc, bias_acc
            )
            out_ref[...] = grad_layer
            low_ref[at, :] = grad_layer.astype(BF)

        @pl.when((index < tiles) & jnp.logical_not(live))
        def _():
            out_ref[...] = jnp.zeros_like(out_ref)
            low_ref[at, :] = jnp.zeros((step, width), BF)

        @pl.when(index >= tiles)
        def _():
            product_block(acc, act_ref, low_ref)
            put_parts_tall(acc, own_ref[0], orders, bounds, outs, index - tiles)

    def row_tile(columns):
        return pl.BlockSpec((step, columns), lambda i, *_: (jnp.minimum(i, tiles - 1), 0))

    out = call(
        kernel,
        [classes, own],
        (tiles + blocks,),
        [whole(v.shape) for v in (*dfq, *back)]
            + [row_tile(width)] * 2
            + [pl.BlockSpec((rows, width), lambda i, *_: (0, jnp.maximum(i - tiles, 0)))]
            + [whole(gains.shape), whole(w_fq.shape)],
        [*dfq, *back, layer, grad, act, gains, w_fq],
        after,
        limit=20,
        out_specs=[row_tile(width)] + [whole_out((1, width))] * 2 + [whole_out(v.shape) for v in outs_shapes],
            scratch=[pltpu.VMEM((rows, width), BF)] * 3 + [pltpu.VMEM((width, width), BF)],
        out_shape=[jax.ShapeDtypeStruct((rows, width), F32)]
        + [jax.ShapeDtypeStruct((1, width), F32)] * 2
        + outs_shapes,
        cost_estimate=cost(2 * rows * width * (width + tall), 16 * rows * width + 2 * act.size + 2 * tall * width),
    )
    return *out[:3], *(Sum(*out[3 + 2 * k : 5 + 2 * k], order) for k, order in enumerate(orders))


def feed_forward_back(grad_layer, up, middle, classes, gains, w_down, w_up, w_out, step, after=()):
    clips = classes.shape[0]
    rows, width = middle.shape
    hidden = w_up.shape[1]
    chunk = width
    blocks = hidden // width

    def kernel(
        cls_ref, g_ref, u_ref, mid_ref, gain_ref, down_w, up_w, out_w,
        gmid_ref, low_ref, do_ref, hid_ref, gain_acc, bias_acc,
    ):
        index = pl.program_id(0)

        @pl.when(index == 0)
        def _():
            gain_acc[...] = jnp.zeros_like(gain_acc)
            bias_acc[...] = jnp.zeros_like(bias_acc)

        live = index * step < total_of(cls_ref, clips)

        @pl.when(live)
        def _():
            grad_layer = g_ref[...]
            down_low = grad_layer.astype(BF)
            total_norm = [jnp.zeros((step, width), F32)]

            def act_stage(k, held):
                held["g"] = dot(down_low, down_w[k * chunk : (k + 1) * chunk, :], 1, 1)

            def slope_stage(k, held):
                part = slice(k * chunk, (k + 1) * chunk)
                value = u_ref[:, part].astype(F32)
                square = value * value
                inner = jnp.tanh(value * (GELU_A + (GELU_A * GELU_B) * square))
                slope = (0.5 + 0.5 * inner) + value * (1.0 - inner * inner) * (
                    0.5 * GELU_A + (1.5 * GELU_A * GELU_B) * square
                )
                held["l"] = (held.pop("g") * slope).astype(BF)
                hid_ref[:, part] = held["l"]

            def norm_stage(k, held):
                total_norm[0] += dot(held.pop("l"), up_w[:, k * chunk : (k + 1) * chunk], 1, 1)

            interleave([act_stage, slope_stage, norm_stage], blocks)
            grad_middle = grad_layer + norm_back(
                mid_ref[...], gain_ref[:, width : 2 * width], total_norm[0], gain_acc, bias_acc
            )
            gmid_ref[...] = grad_middle
            low = grad_middle.astype(BF)
            low_ref[...] = low
            do_ref[...] = dot(low, out_w[...], 1, 1).astype(BF)

        @pl.when(jnp.logical_not(live))
        def _():
            for ref in (gmid_ref, low_ref, do_ref, hid_ref):
                ref[...] = jnp.zeros_like(ref)

    weights = [w_down, w_up, w_out]
    return call(
        kernel,
        [classes],
        (rows // step,),
        [tile(step, width), tile(step, hidden), tile(step, width), whole(gains.shape)]
            + [whole(w.shape) for w in weights],
        [grad_layer, up, middle, gains, *weights],
        after,
        limit=22,
        out_specs=[tile(step, width)] * 3 + [tile(step, hidden)] + [whole_out((1, width))] * 2,
        out_shape=[
            in_hbm((rows, width), F32),
            in_hbm((rows, width), BF),
            jax.ShapeDtypeStruct((rows, width), BF),
            in_hbm((rows, hidden), BF),
        ]
        + [jax.ShapeDtypeStruct((1, width), F32)] * 2,
        cost_estimate=cost(2 * rows * sum(w.size for w in weights), 2 * sum(w.size for w in weights)),
    )


def feed_forward_weights(own, normed, hidden_low, mixed, out_low, shards, orders, cut, after=()):
    rows, width = normed.shape
    blocks = hidden_low.shape[1] // width
    bounds = [0, cut, blocks + 1][: len(orders)] + [blocks + 1]
    specs, shapes = part_outs(shards, width // shards, width, bounds, 0)

    def kernel(own_ref, n_ref, hid_ref, o_ref, low_ref, *refs):
        outs, acc = refs[:-1], refs[-1]
        block = pl.program_id(0)

        @pl.when(block < blocks)
        def _():
            product_block(acc, n_ref, hid_ref)

        @pl.when(block == blocks)
        def _():
            product_block(acc, o_ref, low_ref)

        for kind, order in enumerate(orders):

            @pl.when((block >= bounds[kind]) & (block < bounds[kind + 1]))
            def _():
                put_parts(acc, own_ref[0], shards, order, *outs[2 * kind : 2 * kind + 2])

    out = call(
        kernel,
        [own],
        (blocks + 1,),
        [
                whole(normed.shape),
                pl.BlockSpec((rows, width), lambda j, *_: (0, jnp.minimum(j, blocks - 1))),
                whole(mixed.shape),
                whole(out_low.shape),
            ],
        [normed, hidden_low, mixed, out_low],
        after,
        limit=20,
        out_specs=specs,
            scratch=[pltpu.VMEM((width, width), BF)],
        out_shape=shapes,
        cost_estimate=cost(2 * rows * width * width * (blocks + 1), 2 * rows * width * 8),
    )
    return [Sum(*out[2 * k : 2 * k + 2], order) for k, order in enumerate(orders)]


def self_attend_back(own, qkv, mixed, grad, normed, classes, shards, orders, cut, after=()):
    clips = classes.shape[0]
    rows, wide = qkv.shape
    width = wide // 3
    bounds = [0, cut, 3]
    specs, shapes = part_outs(shards, width // shards, width, bounds, clips)

    def kernel(cls_ref, own_ref, qkv_ref, o_ref, do_ref, n_ref, d_ref, *refs):
        outs = refs[:4]
        acc = refs[4]
        index = pl.program_id(0)

        @pl.when(index < clips)
        def _():
            clip = jnp.minimum(index, clips - 1)
            start = start_dyn(cls_ref, clip, clips)

            def body(count, live):
                at = pl.ds(start, count)

                def columns(part, head):
                    pair = pair_of(head)
                    return slice(part * width + pair.start, part * width + pair.stop)

                def load(part):
                    return lambda head: qkv_ref[at, columns(part, head)]

                def store(head, query, key, value, _):
                    for part, result in enumerate((query, key, value)):
                        d_ref[at, columns(part, head)] = result

                attend_back(
                    load(0),
                    load(1),
                    load(2),
                    lambda head: do_ref[at, pair_of(head)],
                    lambda head: o_ref[at, pair_of(head)],
                    store,
                    live,
                )

            by_class(cls_ref[clip], body)

        @pl.when(index == clips - 1)
        def _():
            clear_tail(cls_ref, clips, [d_ref])

        products = [(n_ref, d_ref.at[:, p * width : (p + 1) * width]) for p in range(3)]
        for block, (left, right) in enumerate(products):

            @pl.when(index == clips + block)
            def _():
                product_block(acc, left, right)
                kind = 0 if block < cut else 1
                put_parts(acc, own_ref[0], shards, orders[kind], *outs[2 * kind : 2 * kind + 2])

    operands = [qkv, mixed, grad, normed]
    out = call(
        kernel,
        [classes, own],
        (clips + 3,),
        [whole(v.shape) for v in operands],
        [*operands],
        after,
        limit=20,
        out_specs=[whole_out((rows, wide))] + specs,
            scratch=[pltpu.VMEM((width, width), BF)],
        out_shape=[jax.ShapeDtypeStruct((rows, wide), BF)] + shapes,
        cost_estimate=cost(48 * rows * MOST * width, 16 * rows * width),
    )
    return out[0], Sum(*out[1:3], orders[0]), Sum(*out[3:5], orders[1])


def norm_project_back(dqkv, x, gmid, classes, gain, weight, step, slots, after=()):
    clips = classes.shape[0]
    rows, width = x.shape
    wide = weight.shape[1]

    def kernel(cls_ref, d_ref, x_ref, gmid_ref, gain_ref, w_ref, out_ref, gain_one, bias_one, packed):
        index = pl.program_id(0)

        @pl.when(index == 0)
        def _():
            gain_one[...] = jnp.zeros_like(gain_one)
            bias_one[...] = jnp.zeros_like(bias_one)

        @pl.when(index * step < total_of(cls_ref, clips))
        def _():
            grad_norm = dot(d_ref[...], w_ref[...], 1, 1)
            at = pl.ds(pl.multiple_of(index * step, 16), step)
            packed[at, :] = gmid_ref[...] + norm_back(
                x_ref[...].astype(F32), gain_ref[:, :width], grad_norm, gain_one, bias_one
            )

        @pl.when(index == rows // step - 1)
        def _():
            for clip in range(clips):
                start = start_of(cls_ref, clip)

                def body(count, live):
                    value = packed[pl.ds(start, count), :]
                    held = min(count, SLOT)
                    first = clip * SLOT
                    out_ref[first : first + held, :] = value[:held]
                    if held < SLOT:
                        out_ref[first + held : first + SLOT, :] = jnp.zeros((SLOT - held, width), F32)

                by_class(cls_ref[clip], body)

    return call(
        kernel,
        [classes],
        (rows // step,),
        [
                tile(step, wide), tile(step, width), tile(step, width), whole(gain.shape), whole(weight.shape),
            ],
        [dqkv, x, gmid, gain, weight],
        after,
        limit=20,
        out_specs=[whole_out((slots, width))] + [whole_out((1, width))] * 2,
            scratch=[pltpu.VMEM((rows, width), F32)],
        out_shape=[jax.ShapeDtypeStruct((slots, width), F32)] + [jax.ShapeDtypeStruct((1, width), F32)] * 2,
        cost_estimate=cost(2 * rows * width * wide, rows * (10 * width + 2 * wide) + 2 * weight.size),
    )


def exchange(value, bit):
    count = lax.axis_size("dp")
    return lax.ppermute(value, "dp", [(i, i ^ (1 << bit)) for i in range(count)])


def tie(values, *before):
    return lax.optimization_barrier((values, before))[0]


class Sum:
    def __init__(self, kept, sent, order):
        self.kept, self.sent, self.order, self.step = kept, sent, order, 0
        self.got = None

    def start(self):
        self.got = exchange(self.sent, self.order[self.step])

    def add(self, *before, go=True):
        if self.step == len(self.order):
            return self.result
        kept, got, self.got = self.kept, self.got, None
        if before:
            kept, got = tie((kept, got), *before)
        self.step += 1
        if self.step == len(self.order):
            self.result = kept[0].astype(F32) + got[0].astype(F32)
            return self.result
        half = kept.shape[0] // 2
        self.sent = (kept[half:].astype(F32) + got[half:].astype(F32)).astype(kept.dtype)
        self.kept = (kept[:half].astype(F32) + got[:half].astype(F32)).astype(kept.dtype)
        if go:
            self.start()
        return self.sent, self.kept


def take_turns(sums, last):
    for one in sums:
        if one.got is None:
            one.start()
        else:
            last = one.add(last)
    return last


def shifted(value, axis, steps):
    count = lax.axis_size(axis)
    return lax.ppermute(value, axis, [(source, (source + steps) % count) for source in range(count)])


def per_device(
    tokens, item_class, norm_gain, norm_bias, attn_qkv, attn_out, mlp_up, mlp_down,
    join_query, join_keyval, join_output, cotangent,
):
    width = tokens.shape[2]
    slots = tokens.shape[1]
    clips = item_class.shape[0]
    rows = clips * MOST
    shards = lax.axis_size("dp")
    step, small_step = MOST, MOST * 2 // 3
    w_qkv, w_out, w_up, w_down = attn_qkv[0], attn_out[0], mlp_up[0], mlp_down[0]
    w_fq, w_fkv, w_fo = join_query[0], join_keyval[0], join_output[0]
    own = lax.axis_index("dp").astype(jnp.int32)[None]

    next_fkv = shifted(w_fkv, "view", -1)
    norm_gain, norm_bias = norm_gain.reshape(1, -1), norm_bias.reshape(1, -1)
    x, low_one, qkv = norm_project(tokens[0], item_class, rows, norm_gain, norm_bias, w_qkv, step)
    mixed = self_attend(qkv, item_class)
    tiles = rows // small_step
    args = (x, mixed, item_class, norm_gain, norm_bias, w_out, w_up, w_down, w_fq, small_step)
    *done, part_a = feed_forward(*args, (0, tiles // 2))
    arrived_a = shifted(part_a, "view", -1)
    *done, part_b = feed_forward(*args, (tiles // 2, tiles), done)
    arrived_b = shifted(part_b, "view", -1)
    middle, low_two, up, act, layer, low_three, fq = done
    grad, grad_mixed = pack_grad(cotangent[0], item_class, rows, w_fo, after=(part_b, arrived_a))

    bits = range(bits_of(shards))
    orders = tuple(bits), (*bits[1::-1], *bits[2:])
    half = clips // 2
    join_args = (fq, grad_mixed, next_fkv, item_class)
    mixed_a, dfq_a, back_a, dkv_a = join_attend((arrived_a,), *join_args, 0, half)
    returned_a = shifted(back_a, "view", 1)
    mixed_b, dfq_b, back_b, dkv_b, arrived = join_attend((arrived_a, arrived_b), *join_args, half, clips, after=back_a)
    returned_b = shifted(back_b, "view", 1)
    join_mixed, dfq = (mixed_a, mixed_b), (dfq_a, dfq_b)
    by_y, by_z = orders
    dkv = (dkv_a, dkv_b)
    join_y = join_weights(
        own, [((arrived,), dkv, 0), ((arrived,), dkv, 1)], item_class, shards, by_y, after=returned_a
    )
    join_y.start()
    join_z = join_weights(
        own, [((low_three,), dfq, 0), (join_mixed, (grad,), 0)], item_class, shards, by_z,
        after=(join_y.kept, returned_b),
    )
    join_z.start()
    joined = join_result(layer, join_mixed, w_fo, item_class, slots, after=join_z.kept)
    grad_layer, gain_three, bias_three, down_y, down_z = join_back(
        own, dfq, (returned_a, returned_b), layer, grad, in_main(act), item_class, norm_gain, w_fq,
        step, shards, orders, (0, width // 2), after=joined,
    )
    down_y.start()
    down_z.start()
    last = [one.add(gain_three) for one in (join_y, join_z)]
    gmid, out_low, do_self, hidden_low, gain_two, bias_two = feed_forward_back(
        grad_layer, in_main(up), middle, item_class, norm_gain, w_down, w_up, w_out, small_step, after=last
    )
    last = [one.add(gain_two, go=False) for one in (join_y, join_z)]
    last += [one.add(gain_two) for one in (down_y, down_z)]
    up_y, up_z = feed_forward_weights(
        own, low_two, in_main(hidden_low), mixed, out_low, shards, orders, 3, after=last
    )
    up_y.start()
    up_z.start()
    join_y.start()
    dqkv, self_y, self_z = self_attend_back(
        own, qkv, mixed, do_self, low_one, item_class, shards, orders, 2, after=up_y.kept
    )
    self_y.start()
    self_z.start()
    last = join_y.add(self_y.kept)
    join_z.start()
    last = [one.add(last, go=False) for one in (down_y, down_z)]
    grad_tokens, gain_one, bias_one = norm_project_back(
        dqkv, x, gmid, item_class, norm_gain, w_qkv, step, slots, after=last
    )
    small = jnp.concatenate([gain_one, gain_two, gain_three, bias_one, bias_two, bias_three], 0)
    small = small.reshape(6, shards, width // shards).transpose(1, 0, 2)
    small = jnp.stack([small[own[0] ^ place_to_part(place, tuple(bits))] for place in range(shards)])
    small = Sum(small[: shards // 2], small[shards // 2 :], tuple(bits))
    last = take_turns(
        (up_z, up_y, join_z, down_y, self_z, self_y, down_y, down_z, up_z, up_y, self_z, self_y, down_z), gain_one
    )
    small.sent = tie(small.sent, last)
    last = take_turns((small, up_z, small, up_y, small, self_z, self_y, small), last)
    for _ in bits[3:]:
        last = [one.add() for one in (join_y, join_z, down_y, down_z, up_y, up_z, self_y, self_z, small)]
    sum_fkv = shifted(tie(join_y.result, gain_one), "view", 1)
    return (
        joined[None],
        grad_tokens[None],
        small.result[None, :3],
        small.result[None, 3:],
        jnp.concatenate([self_y.result, self_z.result], 1)[None],
        up_z.result[None, :, width:],
        jnp.concatenate([up_y.result, up_z.result[:, :width]], 1)[None],
        jnp.concatenate([down_y.result, down_z.result], 1)[None],
        join_z.result[None, :, :width],
        sum_fkv[None],
        join_z.result[None, :, width:],
    )


def solution(mesh):
    weight = P("view", None, None)
    tokens = P("view", "dp", None)
    small = P("view", None, "dp")
    return jax.shard_map(
        per_device,
        mesh=mesh,
        in_specs=(tokens, P("dp")) + (weight,) * 9 + (tokens,),
        out_specs=(tokens, tokens, small, small) + (tokens,) * 7,
        check_vma=False,
    )
```

time: 520 us -> 371 us (0.71)
  waiting for transfers between devices: 207 us -> 79.5 us
  Pallas kernels: 195 us -> 146 us
  starting transfers between devices: 62.2 us -> 99.6 us
  between operations: 14.5 us -> 1.77 us
    unnamed x2 -> x0, waiting for transfers between devices: 66.1 us -> none
    pallas_call x13 -> x15, Pallas kernels: 195 us -> 146 us  [call(): pl.pallas_call(body, grid_spec=pltpu.PrefetchScalarGridSpec(num_scalar_pr...]
    ppermute x12 -> x27, waiting for transfers between devices: 118 us -> 70.3 us  [exchange(): return lax.ppermute(value, 'dp', [(i, i ^ 1 << bit) for i in range(count)])]
    ppermute x12 -> x27, starting transfers between devices: 58.7 us -> 96.2 us  [exchange(): return lax.ppermute(value, 'dp', [(i, i ^ 1 << bit) for i in range(count)])]
    ppermute x4 -> x6, waiting for transfers between devices: 22.4 us -> 9.22 us  [shifted(): lax.ppermute(value, axis, [(source, (source + steps) % count) for source...]
    unnamed x30 -> x119, local copies, waits for them, and re-layouts: 13 us -> 22.1 us
    convert_element_type x8 -> x15, other arithmetic: 11.7 us -> 9.56 us  [the longest x14 9.26 us: add(): (kept[:half].astype(F32) + got[:half].astype(F32)).astype(kept.dtype)]
  transfers between devices with their start and end apart: 17 -> 33, of which waited for: 8 -> 12; matrix products, arithmetic and copies ran while one was open for 6% -> 4% of each run, Pallas kernels for 33% -> 40%
where the time goes in v2:
time: 371 us; the launch traced here: 365 us
  Pallas kernels  146 us (39%)
  starting transfers between devices  99.6 us (27%)
  waiting for transfers between devices  79.5 us (21%)
  local copies, waits for them, and re-layouts  24.4 us (7%)
  other arithmetic  14.2 us (4%)
    pallas_call x15, Pallas kernels, call(): pl.pallas_call(body, grid_spec=pltpu.PrefetchScalarGridSpec(num_scalar_pr...  146 us
    ppermute x27, starting transfers between devices, exchange(): return lax.ppermute(value, 'dp', [(i, i ^ 1 << bit) for i in range(count)])  96.2 us
    ppermute x27, waiting for transfers between devices, exchange(): return lax.ppermute(value, 'dp', [(i, i ^ 1 << bit) for i in range(count)])  70.3 us
    unnamed x119, local copies, waits for them, and re-layouts  22.1 us
    convert_element_type x14, other arithmetic, add(): (kept[:half].astype(F32) + got[:half].astype(F32)).astype(kept.dtype)  9.26 us
    ppermute x6, waiting for transfers between devices, shifted(): lax.ppermute(value, axis, [(source, (source + steps) % count) for source...  9.22 us
  transfers between devices with their start and end apart: 33, of which 12 were waited for; matrix products, arithmetic and copies ran while one was open for 4% of the time, Pallas kernels for 40%

profile of v2, /device:TPU:0, one launch (start us, length us, event | category | flops | bytes accessed | tf_op | source)
XLA Modules:
  0.0 365.3 jit_solution(17969020639127933964)
XLA Ops:
  0.6 2.4 collective-permute-start.1
  3.1 2.0 copy-done.6
  8.7 6.1 %shard_map.203 = (bf16[1344,768]{1,0:T(8,128)(2,1)S(1)}, bf16[1344,768]{1,0:T(8,128)(2,1)}, bf16[1344,2304]{1,0:T(8,128)(2,1)S(1)}) custom-call(s32[4]{0:T(128)S(1)} %copy-done.42, bf16[1296,768]{1,0:T(8,128)(2,1)S(1)} %bitcast.87, f32[1,2304]{1,0:T(1,128)S(1)} %bitcast.88, f32[1,2304]{1,0:T(1,128)S(1)} %bitcast.94, bf16[768,2304]{1,0:T(8,128)(2,1)S(1)} %bitcast.75), custom_call_target="tpu_custom_call" | custom-call | flops 2378170 | bytes 7962 | tf_op jit(solution)/shard_map/pallas_call | solution.py:319
  14.8 4.8 %shard_map.204.refs_2_.refs_3_ = bf16[1344,768]{1,0:T(8,128)(2,1)S(1)} custom-call(s32[4]{0:T(128)S(1)} %copy-done.42, bf16[1344,2304]{1,0:T(8,128)(2,1)S(1)} %get-tuple-element.127.refs_1_.refs_2_), custom_call_target="tpu_custom_call" | custom-call | flops 2774532 | bytes 4128 | tf_op jit(solution)/shard_map/pallas_call | solution.py:319
  19.8 15.4 %shard_map.205 = (f32[1344,768]{1,0:T(8,128)}, bf16[1344,768]{1,0:T(8,128)(2,1)}, bf16[1344,3072]{1,0:T(8,128)(2,1)}, bf16[1344,3072]{1,0:T(8,128)(2,1)}, f32[13...) custom-call(s32[4]{0:T(128)S(1)} %copy-done.42, ...), custom_call_target="tpu_custom_call" | custom-call | flops 3963617 | bytes 15187 | tf_op jit(solution)/shard_map/pallas_call | solution.py:319
  36.0 6.7 %shard_map.206 = (f32[1344,768]{1,0:T(8,128)}, bf16[1344,768]{1,0:T(8,128)(2,1)}, bf16[1344,3072]{1,0:T(8,128)(2,1)}, bf16[1344,3072]{1,0:T(8,128)(2,1)}, f32[13...) custom-call(s32[4]{0:T(128)S(1)} %copy-done.42, ...), custom_call_target="tpu_custom_call", output_to_operand_aliasing={{0}: (9, {}), {1}: (10, {}), {2}: (11, {}), {3}: (12, {}), ... | custom-call | flops 3963617 | bytes 15187 | tf_op jit(solution)/shard_map/pallas_call | solution.py:319
  42.8 5.7 %collective-permute-done.refs_4_.refs_1_ = bf16[672,768]{1,0:T(8,128)(2,1)S(1)} collective-permute-done((bf16[672,768]{1,0:T(8,128)(2,1)}, bf16[672,768]{1,0:T(8,128)(2,1)S(1)}, u32[]{:S(2)}, u32[]{:S(2)}) %collective-permute-start) | collective-permute-done | bytes 1032224 | tf_op jit(solution)/shard_map/ppermute | solution.py:1084
  49.7 3.2 shard_map.207
  53.0 11.3 %shard_map.208 = (bf16[672,768]{1,0:T(8,128)(2,1)}, bf16[672,768]{1,0:T(8,128)(2,1)}, bf16[672,768]{1,0:T(8,128)(2,1)}, bf16[672,1536]{1,0:T(8,128)(2,1)}) custom-call(s32[4]{0:T(128)S(1)} %copy-done.43, bf16[672,768]{1,0:T(8,128)(2,1)S(1)} %collective-permute-done.refs_4_.refs_1_, bf16[1344,768]{1,0:T(8,128)(2,1)S(1)} %copy-done.4, ...), custom_call_target="tpu_custom_call" | custom-call | flops 5549064 | bytes 5160 | tf_op jit(solution)/shard_map/pallas_call | solution.py:319
  64.3 9.4 %shard_map.209 = (bf16[672,768]{1,0:T(8,128)(2,1)}, bf16[672,768]{1,0:T(8,128)(2,1)}, bf16[672,768]{1,0:T(8,128)(2,1)}, bf16[672,1536]{1,0:T(8,128)(2,1)}, bf16[1344,768]{1,0:T(8,128)(2,1)S(1)}) custom-call(s32[4]{0:T(128)S(1)} %copy-done.43, bf16[672,768]{1,0:T(8,128)(2,1)S(1)} %collective-permute-done.refs_4_.refs_1_, ...), custom_call_target="tpu_custom_call" | custom-call | flops 5549064 | bytes 5160 | tf_op jit(solution)/shard_map/pallas_call | solution.py:319
  75.1 3.5 collective-permute-done.3.refs_5_.refs_4_
  78.7 1.6 copy-done.32
  80.2 1.6 copy-done.33
  83.4 5.9 %shard_map.210 = (bf16[4,96,1536]{2,1,0:T(8,128)(2,1)}, bf16[4,96,1536]{2,1,0:T(8,128)(2,1)}) custom-call(s32[4]{0:T(128)S(1)} %copy-done.43, s32[1]{0:T(128)} %bitcast.11.refs_1_.refs_0_, bf16[1344,768]{1,0:T(8,128)(2,1)S(1)} %copy-done.35, bf16[672,1536]{1,0:T(8,128)(2,1)S(1)} %copy-done.32, bf16[672,1536]{1,0:T(8,128)(2,1)S(1)} %copy-done.33, ...), custom_call_target="tpu_custom_call" | custom-call | flops 396361 | bytes 1032 | tf_op jit(solution)/shard_map/pallas_call | solution.py:319
  89.4 26.1 %collective-permute-start.5 = (bf16[4,96,1536]{2,1,0:T(8,128)(2,1)}, bf16[4,96,1536]{2,1,0:T(8,128)(2,1)}, u32[]{:S(2)}, u32[]{:S(2)}) collective-permute-start(bf16[4,96,1536]{2,1,0:T(8,128)(2,1)} %get-tuple-element.157), channel_id=1, source_target_pairs={{0,1},{1,0},{2,3},{3,2},{4,5},{5,4},{6,7},{7,6},{8,9},{9,8},{10,11... | collective-permute-start | bytes 3538952 | tf_op jit(solution)/shard_map/ppermute | solution.py:1040
  118.0 6.0 %shard_map.211 = (bf16[4,96,1536]{2,1,0:T(8,128)(2,1)}, bf16[4,96,1536]{2,1,0:T(8,128)(2,1)}) custom-call(s32[4]{0:T(128)S(1)} %copy-done.43, s32[1]{0:T(128)} %bitcast.11.refs_1_.refs_0_, bf16[1344,768]{1,0:T(8,128)(2,1)S(1)} %copy-done.11, bf16[672,768]{1,0:T(8,128)(2,1)S(1)} %copy-done.25, bf16[672,768]{1,0:T(8,128)(2,1)S(1)} %copy-done.28, ...), custom_call_target="tpu_custom_call" | custom-call | flops 396361 | bytes 1032 | tf_op jit(solution)/shard_map/pallas_call | solution.py:319
  125.3 3.6 shard_map.212.refs_11_
  128.9 1.7 copy-done.15
  130.6 15.2 %shard_map.213 = (f32[1344,768]{1,0:T(8,128)S(1)}, f32[1,768]{1,0:T(1,128)S(1)}, f32[1,768]{1,0:T(1,128)S(1)}, bf16[4,384,384]{2,1,0:T(8,128)(2,1)S(1)}, bf16[4,...) custom-call(s32[4]{0:T(128)S(1)} %copy-done.43, ...), custom_call_target="tpu_custom_call" | custom-call | flops 3963617 | bytes 14745 | tf_op jit(solution)/shard_map/pallas_call | solution.py:319
  145.8 3.3 collective-permute-start.10
  149.1 2.3 collective-permute-start.9
  151.4 1.8 collective-permute-done.6
  153.2 2.4 add_convert_fusion.10
  157.2 21.1 %shard_map.214 = (f32[1344,768]{1,0:T(8,128)}, bf16[1344,768]{1,0:T(8,128)(2,1)}, bf16[1344,768]{1,0:T(8,128)(2,1)S(1)}, bf16[1344,3072]{1,0:T(8,128)(2,1)}, f32[1,768]{1,0:T(1,128)S(1)}, /*index=5*/f32[1,768]{1,0:T(1,128)S(1)}) custom-call(s32[4]{0:T(128)S(1)} %copy-done.43, f32[1344,768]{1,0:T(8,128)S(1)} %get-tuple-element.154.refs_1_, ...), custom_call_target="tpu_custom_call" | custom-call | flops 7134511 | bytes 5308 | tf_op jit(solution)/shard_map/pallas_call | solution.py:319
  178.7 10.9 %collective-permute-start.13 = (bf16[2,384,384]{2,1,0:T(8,128)(2,1)S(1)}, bf16[2,384,384]{2,1,0:T(8,128)(2,1)S(1)}, u32[]{:S(2)}, u32[]{:S(2)}) collective-permute-start(bf16[2,384,384]{2,1,0:T(8,128)(2,1)S(1)} %get-tuple-element.248.refs_11_), channel_id=1, source_target_pairs={{0,1},{1,0},{2,3},{3,2},{4,5},{5,4},{6,7},{7,6},{8,9},{9,8},{10,11... | collective-permute-start | bytes 1769480 | tf_op jit(solution)/shard_map/ppermute | solution.py:1040
  190.1 5.1 %collective-permute-start.12 = (bf16[1,96,1536]{2,1,0:T(8,128)(2,1)S(1)}, bf16[1,96,1536]{2,1,0:T(8,128)(2,1)S(1)}, u32[]{:S(2)}, u32[]{:S(2)}) collective-permute-start(bf16[1,96,1536]{2,1,0:T(8,128)(2,1)S(1)} %get-tuple-element.270.refs_5_), channel_id=1, source_target_pairs={{0,4},{1,5},{2,6},{3,7},{4,0},{5,1},{6,2},{7,3},{8,12},{9,13},{10,... | collective-permute-start | bytes 884744 | tf_op jit(solution)/shard_map/ppermute | solution.py:1040
  195.5 14.1 %shard_map.215 = (bf16[4,96,2304]{2,1,0:T(8,128)(2,1)}, bf16[4,96,2304]{2,1,0:T(8,128)(2,1)}, bf16[4,96,1536]{2,1,0:T(8,128)(2,1)}, bf16[4,96,1536]{2,1,0:T(8,128)(2,1)}) custom-call(s32[1]{0:T(128)} %bitcast.11.refs_1_.refs_0_, bf16[1344,768]{1,0:T(8,128)(2,1)S(1)} %copy-done.12, bf16[1344,3072]{1,0:T(8,128)(2,1)} %get-tuple-element.167.refs_2_, ...), custom_call_target="tpu_custom_call" | custom-call | flops 3963617 | bytes 8257 | tf_op jit(solution)/shard_map/pallas_call | solution.py:319
  211.8 16.4 %shard_map.216 = (bf16[1344,2304]{1,0:T(8,128)(2,1)S(1)}, bf16[4,96,1536]{2,1,0:T(8,128)(2,1)}, bf16[4,96,1536]{2,1,0:T(8,128)(2,1)}, bf16[4,96,768]{2,1,0:T(8,128)(2,1)}, bf16[4,96,768]{2,1,0:T(8,128)(2,1)}) custom-call(s32[4]{0:T(128)S(1)} %copy-done.43, s32[1]{0:T(128)} %bitcast.11.refs_1_.refs_0_, bf16[1344,2304]{1,0:T(8,128)(2,1)S(1)} %bitcast.74, ...), custom_call_target="tpu_custom_call" | custom-call | flops 8323596 | bytes 8257 | tf_op jit(solution)/shard_map/pallas_call | solution.py:319
  230.6 6.6 %shard_map.217 = (f32[1296,768]{1,0:T(8,128)}, f32[1,768]{1,0:T(1,128)S(1)}, f32[1,768]{1,0:T(1,128)S(1)}) custom-call(s32[4]{0:T(128)S(1)} %copy-done.43, bf16[1344,2304]{1,0:T(8,128)(2,1)S(1)} %get-tuple-element.183.refs_1_, bf16[1344,768]{1,0:T(8,128)(2,1)S(1)} %copy-done.3, f32[1344,768]{1,0:T(8,128)S(1)} %copy-done.24, f32[1,2304]{1,0:T(1,128)S(1)} %bitcast.93, ...), custom_call_target="tpu_custom_call" | custom-call | flops 2378170 | bytes 10027 | tf_op jit(solution)/shard_map/pallas_call | solution.py:319
  237.2 7.2 %collective-permute-start.17 = (bf16[1,96,1536]{2,1,0:T(8,128)(2,1)S(1)}, bf16[1,96,1536]{2,1,0:T(8,128)(2,1)S(1)}, u32[]{:S(2)}, u32[]{:S(2)}) collective-permute-start(bf16[1,96,1536]{2,1,0:T(8,128)(2,1)S(1)} %get-tuple-element.268.refs_7_), channel_id=1, source_target_pairs={{0,4},{1,5},{2,6},{3,7},{4,0},{5,1},{6,2},{7,3},{8,12},{9,13},{10,... | collective-permute-start | bytes 884744 | tf_op jit(solution)/shard_map/ppermute | solution.py:1040
  244.4 12.5 %collective-permute-start.16 = (bf16[4,96,768]{2,1,0:T(8,128)(2,1)}, bf16[4,96,768]{2,1,0:T(8,128)(2,1)}, u32[]{:S(2)}, u32[]{:S(2)}) collective-permute-start(bf16[4,96,768]{2,1,0:T(8,128)(2,1)} %get-tuple-element.199), channel_id=1, source_target_pairs={{0,2},{1,3},{2,0},{3,1},{4,6},{5,7},{6,4},{7,5},{8,10},{9,11},{10,... | collective-permute-start | bytes 1769480 | tf_op jit(solution)/shard_map/ppermute | solution.py:1040
  257.2 8.0 %collective-permute-start.15 = (bf16[4,96,1536]{2,1,0:T(8,128)(2,1)}, bf16[4,96,1536]{2,1,0:T(8,128)(2,1)S(1)}, u32[]{:S(2)}, u32[]{:S(2)}) collective-permute-start(bf16[4,96,1536]{2,1,0:T(8,128)(2,1)} %get-tuple-element.197), channel_id=1, source_target_pairs={{0,1},{1,0},{2,3},{3,2},{4,5},{5,4},{6,7},{7,6},{8,9},{9,8},{10,11... | collective-permute-start | bytes 3538952 | tf_op jit(solution)/shard_map/ppermute | solution.py:1040
  265.2 2.0 add_convert_fusion.4
  267.2 3.0 collective-permute-start.14
  270.2 1.9 add_convert_fusion
  272.3 8.9 %collective-permute-done.16 = bf16[4,96,768]{2,1,0:T(8,128)(2,1)} collective-permute-done((bf16[4,96,768]{2,1,0:T(8,128)(2,1)}, bf16[4,96,768]{2,1,0:T(8,128)(2,1)}, u32[]{:S(2)}, u32[]{:S(2)}) %collective-permute-start.16) | collective-permute-done | bytes 589856 | tf_op jit(solution)/shard_map/ppermute | solution.py:1040
  282.4 9.8 %collective-permute-done.15 = bf16[4,96,1536]{2,1,0:T(8,128)(2,1)S(1)} collective-permute-done((bf16[4,96,1536]{2,1,0:T(8,128)(2,1)}, bf16[4,96,1536]{2,1,0:T(8,128)(2,1)S(1)}, u32[]{:S(2)}, u32[]{:S(2)}) %collective-permute-start.15) | collective-permute-done | bytes 1179680 | tf_op jit(solution)/shard_map/ppermute | solution.py:1040
  292.3 2.0 collective-permute-start.21
  294.7 10.2 %collective-permute-done.23 = bf16[2,96,1536]{2,1,0:T(8,128)(2,1)S(1)} collective-permute-done((bf16[2,96,1536]{2,1,0:T(8,128)(2,1)S(1)}, bf16[2,96,1536]{2,1,0:T(8,128)(2,1)S(1)}, u32[]{:S(2)}, u32[]{:S(2)}) %collective-permute-start.23) | collective-permute-done | bytes 589856 | tf_op jit(solution)/shard_map/ppermute | solution.py:1040
  306.0 3.7 %collective-permute-done.22 = bf16[2,96,2304]{2,1,0:T(8,128)(2,1)S(1)} collective-permute-done((bf16[2,96,2304]{2,1,0:T(8,128)(2,1)S(1)}, bf16[2,96,2304]{2,1,0:T(8,128)(2,1)S(1)}, u32[]{:S(2)}, u32[]{:S(2)}) %collective-permute-start.22) | collective-permute-done | bytes 884768 | tf_op jit(solution)/shard_map/ppermute | solution.py:1040
  309.9 7.4 %collective-permute-start.28 = (bf16[1,96,2304]{2,1,0:T(8,128)(2,1)S(1)}, bf16[1,96,2304]{2,1,0:T(8,128)(2,1)S(1)}, u32[]{:S(2)}, u32[]{:S(2)}) collective-permute-start(bf16[1,96,2304]{2,1,0:T(8,128)(2,1)S(1)} %get-tuple-element.256), channel_id=1, source_target_pairs={{0,4},{1,5},{2,6},{3,7},{4,0},{5,1},{6,2},{7,3},{8,12},{9,13},{10,... | collective-permute-start | bytes 1327112 | tf_op jit(solution)/shard_map/ppermute | solution.py:1040
  317.4 10.4 %collective-permute-done.20 = bf16[2,96,1536]{2,1,0:T(8,128)(2,1)S(1)} collective-permute-done((bf16[2,96,1536]{2,1,0:T(8,128)(2,1)S(1)}, bf16[2,96,1536]{2,1,0:T(8,128)(2,1)S(1)}, u32[]{:S(2)}, u32[]{:S(2)}) %collective-permute-start.20) | collective-permute-done | bytes 589856 | tf_op jit(solution)/shard_map/ppermute | solution.py:1040
  327.9 1.9 collective-permute-start.30
  333.0 1.7 collective-permute-done.25
  334.7 2.5 collective-permute-start.27
  337.2 16.3 %collective-permute-done.28 = bf16[1,96,2304]{2,1,0:T(8,128)(2,1)S(1)} collective-permute-done((bf16[1,96,2304]{2,1,0:T(8,128)(2,1)S(1)}, bf16[1,96,2304]{2,1,0:T(8,128)(2,1)S(1)}, u32[]{:S(2)}, u32[]{:S(2)}) %collective-permute-start.28) | collective-permute-done | bytes 442400 | tf_op jit(solution)/shard_map/ppermute | solution.py:1040
  354.8 1.9 collective-permute-done.31
  356.8 5.7 %collective-permute-done.30 = bf16[1,96,1536]{2,1,0:T(8,128)(2,1)S(1)} collective-permute-done((bf16[1,96,1536]{2,1,0:T(8,128)(2,1)S(1)}, bf16[1,96,1536]{2,1,0:T(8,128)(2,1)S(1)}, u32[]{:S(2)}, u32[]{:S(2)}) %collective-permute-start.30) | collective-permute-done | bytes 294944 | tf_op jit(solution)/shard_map/ppermute | solution.py:1040
  (194 shorter events, 30.5 us)
Async XLA Ops:
  0.6 52.3 %collective-permute-start.1 = (bf16[768,1536]{1,0:T(8,128)(2,1)}, bf16[768,1536]{1,0:T(8,128)(2,1)S(1)}, u32[]{:S(2)}, u32[]{:S(2)}) collective-permute-start(bf16[768,1536]{1,0:T(8,128)(2,1)} %bitcast.99), channel_id=1, source_target_pairs={{0,24},{8,0},{16,8},{24,16},{1,25},{9,1},{17,9},{25,17},{2,26},{10... | collective-permute-start | bytes 7077896 | tf_op jit(solution)/shard_map/ppermute | solution.py:1084
  14.8 21.2 %copy-start.2 = (bf16[1344,768]{1,0:T(8,128)(2,1)}, bf16[1344,768]{1,0:T(8,128)(2,1)S(1)}, u32[]{:S(2)}) copy-start(bf16[1344,768]{1,0:T(8,128)(2,1)S(1)} %get-tuple-element.126.refs_1_.refs_2_) | copy-start | bytes 6193156
  35.1 13.3 %collective-permute-start = (bf16[672,768]{1,0:T(8,128)(2,1)}, bf16[672,768]{1,0:T(8,128)(2,1)S(1)}, u32[]{:S(2)}, u32[]{:S(2)}) collective-permute-start(bf16[672,768]{1,0:T(8,128)(2,1)} %get-tuple-element.136), channel_id=1, source_target_pairs={{0,24},{8,0},{16,8},{24,16},{1,25},{9,1},{17,9},{25,17},{2,26},{10... | collective-permute-start | bytes 3096584 | tf_op jit(solution)/shard_map/ppermute | solution.py:1084
  42.7 21.6 %collective-permute-start.2 = (bf16[672,768]{1,0:T(8,128)(2,1)}, bf16[672,768]{1,0:T(8,128)(2,1)S(1)}, u32[]{:S(2)}, u32[]{:S(2)}) collective-permute-start(bf16[672,768]{1,0:T(8,128)(2,1)} %get-tuple-element.138.refs_3_), channel_id=1, source_target_pairs={{0,24},{8,0},{16,8},{24,16},{1,25},{9,1},{17,9},{25,17},{2,26},{10... | collective-permute-start | bytes 3096584 | tf_op jit(solution)/shard_map/ppermute | solution.py:1084
  64.2 14.4 %collective-permute-start.3 = (bf16[672,768]{1,0:T(8,128)(2,1)}, bf16[672,768]{1,0:T(8,128)(2,1)}, u32[]{:S(2)}, u32[]{:S(2)}) collective-permute-start(bf16[672,768]{1,0:T(8,128)(2,1)} %get-tuple-element.141.refs_6_), channel_id=1, source_target_pairs={{0,8},{8,16},{16,24},{24,0},{1,9},{9,17},{17,25},{25,1},{2,10},{10... | collective-permute-start | bytes 3096584 | tf_op jit(solution)/shard_map/ppermute | solution.py:1084
  75.1 40.3 %collective-permute-start.4 = (bf16[672,768]{1,0:T(8,128)(2,1)}, bf16[672,768]{1,0:T(8,128)(2,1)}, u32[]{:S(2)}, u32[]{:S(2)}) collective-permute-start(bf16[672,768]{1,0:T(8,128)(2,1)} %get-tuple-element.151), channel_id=1, source_target_pairs={{0,8},{8,16},{16,24},{24,0},{1,9},{9,17},{17,25},{25,1},{2,10},{10... | collective-permute-start | bytes 3096584 | tf_op jit(solution)/shard_map/ppermute | solution.py:1084
  83.4 32.0 %copy-start.11 = (bf16[1344,768]{1,0:T(8,128)(2,1)S(1)}, bf16[1344,768]{1,0:T(8,128)(2,1)}, u32[]{:S(2)}) copy-start(bf16[1344,768]{1,0:T(8,128)(2,1)} %get-tuple-element.143.refs_2_) | copy-start | bytes 6193156
  83.4 32.0 %copy-start.14 = (bf16[1344,768]{1,0:T(8,128)(2,1)S(1)}, bf16[1344,768]{1,0:T(8,128)(2,1)}, u32[]{:S(2)}) copy-start(bf16[1344,768]{1,0:T(8,128)(2,1)} %copy-done.13) | copy-start | bytes 6193156
  83.4 32.0 %copy-start.25 = (bf16[672,768]{1,0:T(8,128)(2,1)S(1)}, bf16[672,768]{1,0:T(8,128)(2,1)}, u32[]{:S(2)}) copy-start(bf16[672,768]{1,0:T(8,128)(2,1)} %get-tuple-element.144.refs_3_.refs_2_) | copy-start | bytes 3096580
  83.4 32.0 %copy-start.27 = (bf16[672,768]{1,0:T(8,128)(2,1)S(1)}, bf16[672,768]{1,0:T(8,128)(2,1)}, u32[]{:S(2)}) copy-start(bf16[672,768]{1,0:T(8,128)(2,1)} %get-tuple-element.140.refs_5_.refs_2_) | copy-start | bytes 3096580
  83.4 32.0 %copy-start.28 = (bf16[672,768]{1,0:T(8,128)(2,1)S(1)}, bf16[672,768]{1,0:T(8,128)(2,1)}, u32[]{:S(2)}) copy-start(bf16[672,768]{1,0:T(8,128)(2,1)} %get-tuple-element.145.refs_4_.refs_3_) | copy-start | bytes 3096580
  89.4 62.1 %collective-permute-start.5 = (bf16[4,96,1536]{2,1,0:T(8,128)(2,1)}, bf16[4,96,1536]{2,1,0:T(8,128)(2,1)}, u32[]{:S(2)}, u32[]{:S(2)}) collective-permute-start(bf16[4,96,1536]{2,1,0:T(8,128)(2,1)} %get-tuple-element.157), channel_id=1, source_target_pairs={{0,1},{1,0},{2,3},{3,2},{4,5},{5,4},{6,7},{7,6},{8,9},{9,8},{10,11... | collective-permute-start | bytes 3538952 | tf_op jit(solution)/shard_map/ppermute | solution.py:1040
  124.0 29.2 %collective-permute-start.6 = (bf16[4,96,1536]{2,1,0:T(8,128)(2,1)}, bf16[4,96,1536]{2,1,0:T(8,128)(2,1)}, u32[]{:S(2)}, u32[]{:S(2)}) collective-permute-start(bf16[4,96,1536]{2,1,0:T(8,128)(2,1)} %get-tuple-element.161), channel_id=1, source_target_pairs={{0,2},{1,3},{2,0},{3,1},{4,6},{5,7},{6,4},{7,5},{8,10},{9,11},{10,... | collective-permute-start | bytes 3538952 | tf_op jit(solution)/shard_map/ppermute | solution.py:1040
  125.3 31.9 %slice-start.2 = ((s8[4718592]{0:T(1024)(128)(4,1)}), s8[4194304]{0:T(1024)(128)(4,1)S(1)}, s32[]{:S(2)}) async-start(s8[4718592]{0:T(1024)(128)(4,1)} %bitcast.63), calls=%async_computation.2 | async-start | bytes 8388608
  125.3 31.9 %slice-start.6 = ((s8[4718592]{0:T(1024)(128)(4,1)}), s8[4194304]{0:T(1024)(128)(4,1)S(1)}, s32[]{:S(2)}) async-start(s8[4718592]{0:T(1024)(128)(4,1)} %bitcast.70), calls=%async_computation.6 | async-start | bytes 8388608
  130.6 22.6 %copy-start.19 = (bf16[4,96,1536]{2,1,0:T(8,128)(2,1)S(1)}, bf16[4,96,1536]{2,1,0:T(8,128)(2,1)}, u32[]{:S(2)}) copy-start(bf16[4,96,1536]{2,1,0:T(8,128)(2,1)} %get-tuple-element.162.refs_5_) | copy-start | bytes 3538948
  130.6 22.6 %copy-start.23 = (bf16[4,96,1536]{2,1,0:T(8,128)(2,1)S(1)}, bf16[4,96,1536]{2,1,0:T(8,128)(2,1)}, u32[]{:S(2)}) copy-start(bf16[4,96,1536]{2,1,0:T(8,128)(2,1)} %get-tuple-element.159.refs_8_) | copy-start | bytes 3538948
  130.6 26.6 %slice-start.3 = ((s8[4718592]{0:T(1024)(128)(4,1)}), s8[524288]{0:T(1024)(128)(4,1)S(1)}, s32[]{:S(2)}) async-start(s8[4718592]{0:T(1024)(128)(4,1)} %bitcast.63), calls=%async_computation.3 | async-start | bytes 1048576
  130.6 26.6 %slice-start.7 = ((s8[4718592]{0:T(1024)(128)(4,1)}), s8[524288]{0:T(1024)(128)(4,1)S(1)}, s32[]{:S(2)}) async-start(s8[4718592]{0:T(1024)(128)(4,1)} %bitcast.70), calls=%async_computation.7 | async-start | bytes 1048576
  145.8 32.5 %collective-permute-start.10 = (bf16[4,384,384]{2,1,0:T(8,128)(2,1)S(1)}, bf16[4,384,384]{2,1,0:T(8,128)(2,1)S(1)}, u32[]{:S(2)}, u32[]{:S(2)}) collective-permute-start(bf16[4,384,384]{2,1,0:T(8,128)(2,1)S(1)} %get-tuple-element.179), channel_id=1, source_target_pairs={{0,2},{1,3},{2,0},{3,1},{4,6},{5,7},{6,4},{7,5},{8,10},{9,11},{10,... | collective-permute-start | bytes 3538952 | tf_op jit(solution)/shard_map/ppermute | solution.py:1040
  149.1 29.2 %collective-permute-start.9 = (bf16[4,384,384]{2,1,0:T(8,128)(2,1)S(1)}, bf16[4,384,384]{2,1,0:T(8,128)(2,1)S(1)}, u32[]{:S(2)}, u32[]{:S(2)}) collective-permute-start(bf16[4,384,384]{2,1,0:T(8,128)(2,1)S(1)} %get-tuple-element.175), channel_id=1, source_target_pairs={{0,1},{1,0},{2,3},{3,2},{4,5},{5,4},{6,7},{7,6},{8,9},{9,8},{10,11... | collective-permute-start | bytes 3538952 | tf_op jit(solution)/shard_map/ppermute | solution.py:1040
  155.6 34.4 %collective-permute-start.8 = (bf16[2,96,1536]{2,1,0:T(8,128)(2,1)S(1)}, bf16[2,96,1536]{2,1,0:T(8,128)(2,1)S(1)}, u32[]{:S(2)}, u32[]{:S(2)}) collective-permute-start(bf16[2,96,1536]{2,1,0:T(8,128)(2,1)S(1)} %get-tuple-element.252.refs_10_), channel_id=1, source_target_pairs={{0,1},{1,0},{2,3},{3,2},{4,5},{5,4},{6,7},{7,6},{8,9},{9,8},{10,11... | collective-permute-start | bytes 1769480 | tf_op jit(solution)/shard_map/ppermute | solution.py:1040
  156.9 33.1 %collective-permute-start.7 = (bf16[2,96,1536]{2,1,0:T(8,128)(2,1)S(1)}, bf16[2,96,1536]{2,1,0:T(8,128)(2,1)S(1)}, u32[]{:S(2)}, u32[]{:S(2)}) collective-permute-start(bf16[2,96,1536]{2,1,0:T(8,128)(2,1)S(1)} %get-tuple-element.291.refs_8_), channel_id=1, source_target_pairs={{0,2},{1,3},{2,0},{3,1},{4,6},{5,7},{6,4},{7,5},{8,10},{9,11},{10,... | collective-permute-start | bytes 1769480 | tf_op jit(solution)/shard_map/ppermute | solution.py:1040
  178.7 50.4 %collective-permute-start.13 = (bf16[2,384,384]{2,1,0:T(8,128)(2,1)S(1)}, bf16[2,384,384]{2,1,0:T(8,128)(2,1)S(1)}, u32[]{:S(2)}, u32[]{:S(2)}) collective-permute-start(bf16[2,384,384]{2,1,0:T(8,128)(2,1)S(1)} %get-tuple-element.248.refs_11_), channel_id=1, source_target_pairs={{0,1},{1,0},{2,3},{3,2},{4,5},{5,4},{6,7},{7,6},{8,9},{9,8},{10,11... | collective-permute-start | bytes 1769480 | tf_op jit(solution)/shard_map/ppermute | solution.py:1040
  189.9 39.1 %collective-permute-start.11 = (bf16[2,384,384]{2,1,0:T(8,128)(2,1)S(1)}, bf16[2,384,384]{2,1,0:T(8,128)(2,1)S(1)}, u32[]{:S(2)}, u32[]{:S(2)}) collective-permute-start(bf16[2,384,384]{2,1,0:T(8,128)(2,1)S(1)} %get-tuple-element.250.refs_9_), channel_id=1, source_target_pairs={{0,2},{1,3},{2,0},{3,1},{4,6},{5,7},{6,4},{7,5},{8,10},{9,11},{10,... | collective-permute-start | bytes 1769480 | tf_op jit(solution)/shard_map/ppermute | solution.py:1040
  190.1 38.0 %collective-permute-start.12 = (bf16[1,96,1536]{2,1,0:T(8,128)(2,1)S(1)}, bf16[1,96,1536]{2,1,0:T(8,128)(2,1)S(1)}, u32[]{:S(2)}, u32[]{:S(2)}) collective-permute-start(bf16[1,96,1536]{2,1,0:T(8,128)(2,1)S(1)} %get-tuple-element.270.refs_5_), channel_id=1, source_target_pairs={{0,4},{1,5},{2,6},{3,7},{4,0},{5,1},{6,2},{7,3},{8,12},{9,13},{10,... | collective-permute-start | bytes 884744 | tf_op jit(solution)/shard_map/ppermute | solution.py:1040
  209.6 55.6 %collective-permute-start.19 = (bf16[4,96,1536]{2,1,0:T(8,128)(2,1)}, bf16[4,96,1536]{2,1,0:T(8,128)(2,1)}, u32[]{:S(2)}, u32[]{:S(2)}) collective-permute-start(bf16[4,96,1536]{2,1,0:T(8,128)(2,1)} %get-tuple-element.202), channel_id=1, source_target_pairs={{0,2},{1,3},{2,0},{3,1},{4,6},{5,7},{6,4},{7,5},{8,10},{9,11},{10,... | collective-permute-start | bytes 3538952 | tf_op jit(solution)/shard_map/ppermute | solution.py:1040
  209.6 57.6 %collective-permute-start.18 = (bf16[4,96,2304]{2,1,0:T(8,128)(2,1)}, bf16[4,96,2304]{2,1,0:T(8,128)(2,1)}, u32[]{:S(2)}, u32[]{:S(2)}) collective-permute-start(bf16[4,96,2304]{2,1,0:T(8,128)(2,1)} %get-tuple-element.200), channel_id=1, source_target_pairs={{0,1},{1,0},{2,3},{3,2},{4,5},{5,4},{6,7},{7,6},{8,9},{9,8},{10,11... | collective-permute-start | bytes 5308424 | tf_op jit(solution)/shard_map/ppermute | solution.py:1040
  211.7 17.6 %copy-start.7 = (bf16[1,768,2304]{2,1,0:T(8,128)(2,1)S(1)}, bf16[1,768,2304]{2,1,0:T(8,128)(2,1)}, u32[]{:S(2)}) copy-start(bf16[1,768,2304]{2,1,0:T(8,128)(2,1)} %param.16) | copy-start | bytes 10616836
  211.7 17.6 %copy-start.24 = (f32[1344,768]{1,0:T(8,128)S(1)}, f32[1344,768]{1,0:T(8,128)}, u32[]{:S(2)}) copy-start(f32[1344,768]{1,0:T(8,128)} %get-tuple-element.184.refs_3_) | copy-start | bytes 12386308
  237.2 20.0 %collective-permute-start.32 = (f32[96,1536]{1,0:T(8,128)}, f32[96,1536]{1,0:T(8,128)S(1)}, u32[]{:S(2)}, u32[]{:S(2)}) collective-permute-start(f32[96,1536]{1,0:T(8,128)} %add_bitcast_fusion.6), channel_id=1, source_target_pairs={{0,8},{8,16},{16,24},{24,0},{1,9},{9,17},{17,25},{25,1},{2,10},{10... | collective-permute-start | bytes 1769480 | tf_op jit(solution)/shard_map/ppermute | solution.py:1084
  237.2 34.9 %collective-permute-start.17 = (bf16[1,96,1536]{2,1,0:T(8,128)(2,1)S(1)}, bf16[1,96,1536]{2,1,0:T(8,128)(2,1)S(1)}, u32[]{:S(2)}, u32[]{:S(2)}) collective-permute-start(bf16[1,96,1536]{2,1,0:T(8,128)(2,1)S(1)} %get-tuple-element.268.refs_7_), channel_id=1, source_target_pairs={{0,4},{1,5},{2,6},{3,7},{4,0},{5,1},{6,2},{7,3},{8,12},{9,13},{10,... | collective-permute-start | bytes 884744 | tf_op jit(solution)/shard_map/ppermute | solution.py:1040
  244.4 36.8 %collective-permute-start.16 = (bf16[4,96,768]{2,1,0:T(8,128)(2,1)}, bf16[4,96,768]{2,1,0:T(8,128)(2,1)}, u32[]{:S(2)}, u32[]{:S(2)}) collective-permute-start(bf16[4,96,768]{2,1,0:T(8,128)(2,1)} %get-tuple-element.199), channel_id=1, source_target_pairs={{0,2},{1,3},{2,0},{3,1},{4,6},{5,7},{6,4},{7,5},{8,10},{9,11},{10,... | collective-permute-start | bytes 1769480 | tf_op jit(solution)/shard_map/ppermute | solution.py:1040
  257.2 35.1 %collective-permute-start.15 = (bf16[4,96,1536]{2,1,0:T(8,128)(2,1)}, bf16[4,96,1536]{2,1,0:T(8,128)(2,1)S(1)}, u32[]{:S(2)}, u32[]{:S(2)}) collective-permute-start(bf16[4,96,1536]{2,1,0:T(8,128)(2,1)} %get-tuple-element.197), channel_id=1, source_target_pairs={{0,1},{1,0},{2,3},{3,2},{4,5},{5,4},{6,7},{7,6},{8,9},{9,8},{10,11... | collective-permute-start | bytes 3538952 | tf_op jit(solution)/shard_map/ppermute | solution.py:1040
  265.2 29.4 %collective-permute-start.24 = (bf16[1,384,384]{2,1,0:T(8,128)(2,1)S(1)}, bf16[1,384,384]{2,1,0:T(8,128)(2,1)S(1)}, u32[]{:S(2)}, u32[]{:S(2)}) collective-permute-start(bf16[1,384,384]{2,1,0:T(8,128)(2,1)S(1)} %get-tuple-element.266.refs_6_), channel_id=1, source_target_pairs={{0,4},{1,5},{2,6},{3,7},{4,0},{5,1},{6,2},{7,3},{8,12},{9,13},{10,... | collective-permute-start | bytes 884744 | tf_op jit(solution)/shard_map/ppermute | solution.py:1040
  267.2 62.6 %collective-permute-start.14 = (bf16[1,384,384]{2,1,0:T(8,128)(2,1)S(1)}, bf16[1,384,384]{2,1,0:T(8,128)(2,1)S(1)}, u32[]{:S(2)}, u32[]{:S(2)}) collective-permute-start(bf16[1,384,384]{2,1,0:T(8,128)(2,1)S(1)} %get-tuple-element.264.refs_8_), channel_id=1, source_target_pairs={{0,4},{1,5},{2,6},{3,7},{4,0},{5,1},{6,2},{7,3},{8,12},{9,13},{10,... | collective-permute-start | bytes 884744 | tf_op jit(solution)/shard_map/ppermute | solution.py:1040
  272.1 32.8 %collective-permute-start.23 = (bf16[2,96,1536]{2,1,0:T(8,128)(2,1)S(1)}, bf16[2,96,1536]{2,1,0:T(8,128)(2,1)S(1)}, u32[]{:S(2)}, u32[]{:S(2)}) collective-permute-start(bf16[2,96,1536]{2,1,0:T(8,128)(2,1)S(1)} %get-tuple-element.246), channel_id=1, source_target_pairs={{0,1},{1,0},{2,3},{3,2},{4,5},{5,4},{6,7},{7,6},{8,9},{9,8},{10,11... | collective-permute-start | bytes 1769480 | tf_op jit(solution)/shard_map/ppermute | solution.py:1040
  272.3 22.0 %copy-start.45 = (bf16[4,96,1536]{2,1,0:T(8,128)(2,1)S(1)}, bf16[4,96,1536]{2,1,0:T(8,128)(2,1)}, u32[]{:S(2)}) copy-start(bf16[4,96,1536]{2,1,0:T(8,128)(2,1)} %get-tuple-element.211) | copy-start | bytes 3538948
  281.2 28.4 %collective-permute-start.22 = (bf16[2,96,2304]{2,1,0:T(8,128)(2,1)S(1)}, bf16[2,96,2304]{2,1,0:T(8,128)(2,1)S(1)}, u32[]{:S(2)}, u32[]{:S(2)}) collective-permute-start(bf16[2,96,2304]{2,1,0:T(8,128)(2,1)S(1)} %get-tuple-element.242), channel_id=1, source_target_pairs={{0,2},{1,3},{2,0},{3,1},{4,6},{5,7},{6,4},{7,5},{8,10},{9,11},{10,... | collective-permute-start | bytes 2654216 | tf_op jit(solution)/shard_map/ppermute | solution.py:1040
  292.3 25.0 %collective-permute-start.21 = (bf16[2,96,768]{2,1,0:T(8,128)(2,1)S(1)}, bf16[2,96,768]{2,1,0:T(8,128)(2,1)S(1)}, u32[]{:S(2)}, u32[]{:S(2)}) collective-permute-start(bf16[2,96,768]{2,1,0:T(8,128)(2,1)S(1)} %get-tuple-element.262), channel_id=1, source_target_pairs={{0,1},{1,0},{2,3},{3,2},{4,5},{5,4},{6,7},{7,6},{8,9},{9,8},{10,11... | collective-permute-start | bytes 884744 | tf_op jit(solution)/shard_map/ppermute | solution.py:1040
  294.6 33.2 %collective-permute-start.20 = (bf16[2,96,1536]{2,1,0:T(8,128)(2,1)S(1)}, bf16[2,96,1536]{2,1,0:T(8,128)(2,1)S(1)}, u32[]{:S(2)}, u32[]{:S(2)}) collective-permute-start(bf16[2,96,1536]{2,1,0:T(8,128)(2,1)S(1)} %get-tuple-element.243), channel_id=1, source_target_pairs={{0,2},{1,3},{2,0},{3,1},{4,6},{5,7},{6,4},{7,5},{8,10},{9,11},{10,... | collective-permute-start | bytes 1769480 | tf_op jit(solution)/shard_map/ppermute | solution.py:1040
  305.0 25.9 %collective-permute-start.26 = (bf16[1,96,1536]{2,1,0:T(8,128)(2,1)S(1)}, bf16[1,96,1536]{2,1,0:T(8,128)(2,1)S(1)}, u32[]{:S(2)}, u32[]{:S(2)}) collective-permute-start(bf16[1,96,1536]{2,1,0:T(8,128)(2,1)S(1)} %get-tuple-element.260), channel_id=1, source_target_pairs={{0,4},{1,5},{2,6},{3,7},{4,0},{5,1},{6,2},{7,3},{8,12},{9,13},{10,... | collective-permute-start | bytes 884744 | tf_op jit(solution)/shard_map/ppermute | solution.py:1040
  309.9 43.7 %collective-permute-start.28 = (bf16[1,96,2304]{2,1,0:T(8,128)(2,1)S(1)}, bf16[1,96,2304]{2,1,0:T(8,128)(2,1)S(1)}, u32[]{:S(2)}, u32[]{:S(2)}) collective-permute-start(bf16[1,96,2304]{2,1,0:T(8,128)(2,1)S(1)} %get-tuple-element.256), channel_id=1, source_target_pairs={{0,4},{1,5},{2,6},{3,7},{4,0},{5,1},{6,2},{7,3},{8,12},{9,13},{10,... | collective-permute-start | bytes 1327112 | tf_op jit(solution)/shard_map/ppermute | solution.py:1040
  317.3 39.4 %collective-permute-start.31 = (bf16[1,96,768]{2,1,0:T(8,128)(2,1)S(1)}, bf16[1,96,768]{2,1,0:T(8,128)(2,1)S(1)}, u32[]{:S(2)}, u32[]{:S(2)}) collective-permute-start(bf16[1,96,768]{2,1,0:T(8,128)(2,1)S(1)} %get-tuple-element.276), channel_id=1, source_target_pairs={{0,4},{1,5},{2,6},{3,7},{4,0},{5,1},{6,2},{7,3},{8,12},{9,13},{10,... | collective-permute-start | bytes 442376 | tf_op jit(solution)/shard_map/ppermute | solution.py:1040
  327.9 34.5 %collective-permute-start.30 = (bf16[1,96,1536]{2,1,0:T(8,128)(2,1)S(1)}, bf16[1,96,1536]{2,1,0:T(8,128)(2,1)S(1)}, u32[]{:S(2)}, u32[]{:S(2)}) collective-permute-start(bf16[1,96,1536]{2,1,0:T(8,128)(2,1)S(1)} %get-tuple-element.258), channel_id=1, source_target_pairs={{0,4},{1,5},{2,6},{3,7},{4,0},{5,1},{6,2},{7,3},{8,12},{9,13},{10,... | collective-permute-start | bytes 884744 | tf_op jit(solution)/shard_map/ppermute | solution.py:1040
  331.0 3.7 %collective-permute-start.25 = (f32[4,6,96]{2,0,1:T(4,128)S(1)}, f32[4,6,96]{2,0,1:T(4,128)S(1)}, u32[]{:S(2)}, u32[]{:S(2)}) collective-permute-start(f32[4,6,96]{2,0,1:T(4,128)S(1)} %pad_maximum_fusion.1), channel_id=1, source_target_pairs={{0,1},{1,0},{2,3},{3,2},{4,5},{5,4},{6,7},{7,6},{8,9},{9,8},{10,11... | collective-permute-start | bytes 27656 | tf_op jit(solution)/shard_map/ppermute | solution.py:1040
  334.7 20.1 %collective-permute-start.27 = (f32[2,6,96]{2,0,1:T(2,128)S(1)}, f32[2,6,96]{2,0,1:T(2,128)S(1)}, u32[]{:S(2)}, u32[]{:S(2)}) collective-permute-start(f32[2,6,96]{2,0,1:T(2,128)S(1)} %get-tuple-element.277), channel_id=1, source_target_pairs={{0,2},{1,3},{2,0},{3,1},{4,6},{5,7},{6,4},{7,5},{8,10},{9,11},{10,... | collective-permute-start | bytes 13832 | tf_op jit(solution)/shard_map/ppermute | solution.py:1040
  354.8 8.7 %collective-permute-start.29 = (f32[1,6,96]{2,0,1:T(1,128)S(1)}, f32[1,6,96]{2,0,1:T(1,128)S(1)}, u32[]{:S(2)}, u32[]{:S(2)}) collective-permute-start(f32[1,6,96]{2,0,1:T(1,128)S(1)} %get-tuple-element.287), channel_id=1, source_target_pairs={{0,4},{1,5},{2,6},{3,7},{4,0},{5,1},{6,2},{7,3},{8,12},{9,13},{10,... | collective-permute-start | bytes 6920 | tf_op jit(solution)/shard_map/ppermute | solution.py:1040
  (44 other events, 225.0 us)
